TPU v7x, 32 devices: a whole 2x2x4 slice. The times are simulated.
32 devices in a mesh: ctx: 8 (over z, x), head: 4 (over y, core).
Axes of the slice: x: 2, y: 2, z: 4, core: 2. Of those that a mesh axis runs over, the one named last changes fastest.
Arguments:
- hidden_in: bfloat16 [4096, 7168], P('ctx', 'head'), may hold values from -6 to 6
- gate_weight: bfloat16 [7168, 192], P('head'), may hold values from -0.09375 to 0.09375
- encoded_queries: bfloat16 [4096, 64, 128], P('ctx', 'head'), may hold values from -12 to 12
- encoded_keys: bfloat16 [4096, 4, 128], P('ctx', 'head'), may hold values from -12 to 12
- value_tensor: bfloat16 [4096, 4, 128], P('ctx', 'head'), may hold values from -6 to 6
- comp_key_weight: float32 [64, 128], replicated, may hold values from -0.75 to 0.75
- comp_value_weight: float32 [64, 128], replicated, may hold values from -0.75 to 0.75
- selection: int32 [64, 4, 16], P('ctx', 'head'), may hold values from 0 to 63, as said below
Outputs:
- attended: bfloat16 [4096, 64, 128], P('ctx', 'head')
Inputs may be any that keep to these rules, and one draw needn't show every extreme that they name: `selection`: entries of one list are distinct and the first is the query block's own block. For one index of ctx and one group, the blocks named over all its query blocks that lie in one other index's shard are at most 4, and some index reaches 4 in every draw.
All inputs are finite; a program needn't handle non-finite values.
Results may differ from a plain program's by a relative error of at most 0.011.
Values may be sent and summed in bfloat16 or wider, within the bound.
A program may use at most 64 MiB of HBM per device.

v0:
```python
import jax
import jax.numpy as jnp
from jax import lax
from jax.sharding import PartitionSpec as P

WINDOW_TOKENS = 512


def shifted(value, axis, steps):
    count = lax.axis_size(axis)
    initial, last = (max(0, -steps), min(count, count - steps))
    return lax.ppermute(value, axis, [(source, source + steps) for source in range(initial, last)])


def attend(query_block_index, key_rows, value_rows, key_mask, with_null):
    scale = query_block_index.shape[-1] ** (-0.5)
    if key_rows.dtype == jnp.float32:
        scores = (
            jnp.einsum(
                "tgjd,gkd->tgjk",
                query_block_index.astype(jnp.float32),
                key_rows,
                preferred_element_type=jnp.float32,
                precision=lax.Precision.HIGHEST,
            )
            * scale
        )
    else:
        scores = (
            jnp.einsum(
                "tgjd,gkd->tgjk", query_block_index, key_rows, preferred_element_type=jnp.float32
            )
            * scale
        )
    scores = jnp.where(key_mask[:, :, None, :], scores, -1e30)
    peak = jnp.max(scores, axis=-1, keepdims=True)
    if with_null:
        peak = jnp.maximum(peak, 0.0)
    weights = jnp.exp(scores - peak)
    total_w = jnp.sum(weights, axis=-1, keepdims=True)
    if with_null:
        total_w = total_w + jnp.exp(-peak)
    rounded = (weights / total_w).astype(jnp.bfloat16)
    if value_rows.dtype == jnp.float32:
        return jnp.einsum(
            "tgjk,gkd->tgjd",
            rounded.astype(jnp.float32),
            value_rows,
            preferred_element_type=jnp.float32,
            precision=lax.Precision.HIGHEST,
        )
    return jnp.einsum("tgjk,gkd->tgjd", rounded, value_rows, preferred_element_type=jnp.float32)


def body(
    hidden_in,
    gate_weight,
    encoded_queries,
    encoded_keys,
    value_tensor,
    comp_key_weight,
    comp_value_weight,
    selection,
):
    rows_here, heads_here, head_dim = encoded_queries.shape
    block_len = comp_key_weight.shape[0]
    top_count = selection.shape[-1]
    blocks_here = rows_here // block_len
    shard_parts = lax.axis_size("ctx")
    own_index = lax.axis_index("ctx")
    block_count_total = blocks_here * shard_parts
    window_len = WINDOW_TOKENS
    partial_value = jnp.dot(hidden_in, gate_weight, preferred_element_type=jnp.float32)
    logits = lax.psum_scatter(partial_value, "head", scatter_dimension=1, tiled=True)
    gate_values = jax.nn.sigmoid(logits).reshape(rows_here, 1, heads_here, 3)
    key_value = jnp.concatenate([encoded_keys, value_tensor], axis=-1).reshape(
        rows_here, 2 * head_dim
    )
    widened = key_value.astype(jnp.float32).reshape(blocks_here, block_len, 2 * head_dim)
    compress_w = jnp.concatenate([comp_key_weight, comp_value_weight], axis=-1)
    summary = jnp.sum(widened * compress_w[None, :, :], axis=1)
    summaries = lax.all_gather(summary, "ctx", axis=0, tiled=True)
    previous = shifted(key_value, "ctx", 1)
    extended = jnp.concatenate([previous, key_value], axis=0)
    blocks = key_value.reshape(blocks_here, block_len, 2 * head_dim)
    chosen_blocks = selection[:, 0, :]
    all_ids = jnp.arange(block_count_total, dtype=jnp.int32)
    all_blocks = lax.all_gather(blocks, "ctx", axis=0, tiled=True)
    picked = jnp.take(all_blocks, chosen_blocks, axis=0)
    offset = own_index * rows_here
    comp_ends = (all_ids + 1) * block_len - 1
    inner_result = jnp.arange(block_len, dtype=jnp.int32)
    comp_keys = summaries[None, :, :head_dim]
    comp_values = summaries[None, :, head_dim:]

    def per_block(block_num):
        query_start = block_num * block_len
        query_block_index = lax.dynamic_slice_in_dim(
            encoded_queries, query_start, block_len, 0
        ).reshape(block_len, 1, heads_here, head_dim)
        query_pos = offset + query_start + inner_result
        comp_mask = (comp_ends[None, :] <= query_pos[:, None])[:, None, :]
        out_comp = attend(query_block_index, comp_keys, comp_values, comp_mask, True)
        sel_tiles = lax.dynamic_index_in_dim(picked, block_num, 0, keepdims=False).reshape(
            top_count * block_len, 2 * head_dim
        )
        sel_ids = lax.dynamic_index_in_dim(chosen_blocks, block_num, 0, keepdims=False)
        selected_positions = (sel_ids[:, None] * block_len + inner_result[None, :]).reshape(-1)
        sel_mask = (selected_positions[None, :] <= query_pos[:, None])[:, None, :]
        out_sel = attend(
            query_block_index,
            sel_tiles[None, :, :head_dim],
            sel_tiles[None, :, head_dim:],
            sel_mask,
            False,
        )
        win_rows = lax.dynamic_slice_in_dim(extended, query_start, window_len + block_len, 0)
        win_pos = (
            offset + query_start - window_len + jnp.arange(window_len + block_len, dtype=jnp.int32)
        )
        win_mask = (
            (win_pos[None, :] <= query_pos[:, None])
            & (win_pos[None, :] > query_pos[:, None] - window_len)
            & (win_pos[None, :] >= 0)
        )
        out_win = attend(
            query_block_index,
            win_rows[None, :, :head_dim],
            win_rows[None, :, head_dim:],
            win_mask[:, None, :],
            False,
        )
        gate_block_rows = lax.dynamic_slice_in_dim(gate_values, query_start, block_len, 0)
        merged = (
            gate_block_rows[..., 0:1] * out_comp
            + gate_block_rows[..., 1:2] * out_sel
            + gate_block_rows[..., 2:3] * out_win
        )
        return merged.reshape(block_len, heads_here, head_dim).astype(jnp.bfloat16)

    results = lax.map(per_block, jnp.arange(blocks_here, dtype=jnp.int32))
    return results.reshape(rows_here, heads_here, head_dim)


def solution(mesh):
    return jax.shard_map(
        body,
        mesh=mesh,
        in_specs=(
            P("ctx", "head"),
            P("head", None),
            P("ctx", "head", None),
            P("ctx", "head", None),
            P("ctx", "head", None),
            P(),
            P(),
            P("ctx", "head", None),
        ),
        out_specs=P("ctx", "head", None),
        check_vma=False,
    )
```

profile of v0, /device:TPU:0, one launch (start us, length us, event | category | flops | bytes accessed | tf_op | source)
XLA Modules:
  0.0 259.7 jit_solution(10590901682099796140)
XLA Ops:
  8.9 2.6 %fusion.57 = f32[512,192]{0,1:T(8,128)} fusion(bf16[512,1792]{1,0:T(8,128)(2,1)S(1)} %copy-done, bf16[1792,192]{0,1:T(8,128)(2,1)} %param.11), kind=kOutput, calls=%fused_computation.82 | convolution fusion | flops 352321536 | bytes 2916352 | tf_op jit(solution)/shard_map/dot_general | solution.py:73
  12.4 4.9 %collective-permute-start = (bf16[512,256]{1,0:T(8,128)(2,1)}, bf16[512,256]{1,0:T(8,128)(2,1)S(1)}, u32[]{:S(2)}, u32[]{:S(2)}) collective-permute-start(bf16[512,256]{1,0:T(8,128)(2,1)} %bitcast.175), channel_id=1, source_target_pairs={{0,4},{4,8},{8,12},{12,16},{16,20},{20,24},{24,28},{1,5},{5,9},{9,... | collective-permute-start | bytes 786440 | tf_op jit(solution)/shard_map/ppermute | solution.py:12
  18.4 31.0 %all_gather.6 = f32[64,256]{1,0:T(8,128)S(1)} all-gather(f32[8,256]{1,0:T(8,128)S(1)} %multiply_reduce_fusion), channel_id=1, replica_groups=mesh['ctx'=8,'head'=4] {'ctx'}, dimensions={0}, use_global_device_ids=true | all-gather | bytes 73728 | tf_op jit(solution)/shard_map/all_gather | solution.py:82
  49.4 1.8 pad_maximum_fusion
  52.9 13.4 %all-gather.2.cloned.1.call-done = bf16[64,64,256]{2,1,0:T(8,128)(2,1)} async-done(((bf16[8,64,256]{2,1,0:T(8,128)(2,1)}), bf16[64,64,256]{2,1,0:T(8,128)(2,1)}) %all-gather.2.cloned.1.call-update) | async-done | bytes 2097168 | tf_op jit(solution)/shard_map/all_gather | solution.py:88
  66.3 4.4 %gather_fusion = bf16[128,64,256]{2,1,0:T(8,128)(2,1)} fusion(bf16[64,64,256]{2,1,0:T(8,128)(2,1)} %all-gather.2.cloned.1.call-done, s32[1024]{0:T(1024)S(1)} %pad_clamp_fusion), kind=kCustom, calls=%fused_computation | custom fusion | bytes 8389120 | tf_op jit(solution)/shard_map/jit(_take)/gather | solution.py:89
  70.7 4.6 %broadcast_select_fusion = bf16[8,16,64,256]{3,2,1,0:T(8,128)(2,1)} fusion(bf16[8,16,64,256]{3,2,1,0:T(8,128)(2,1)} %bitcast.173, pred[8,16]{1,0:T(8,128)(4,1)S(1)} %compare_and_fusion), kind=kLoop, calls=%fused_computation.68 | loop fusion | flops 2097152 | bytes 8388736 | tf_op jit(solution)/shard_map/jit(_take)/select_n | solution.py:89
  75.2 177.1 %while.15 = (s32[]{:T(128)}, bf16[8,64,16,128]{3,2,1,0:T(8,128)(2,1)}, s32[8]{0:T(128)S(1)}, f32[512,1,16,3]{0,3,2,1:T(4,128)}, s32[]{:T(128)}, /*index=5*/bf16[...) while((s32[]{:T(128)}, ...), condition=%wide.region_9.10_spmd.clone.clone, body=%wide.region_2.9_spmd.clone.clone.sunk | while | flops 1061377024 | bytes 33218792 | solution.py:141
  85.5 2.1 fusion.89
  87.6 3.7 %fusion.90 = f32[1,128,64,16]{1,3,2,0:T(8,128)} fusion(f32[1,128,64,16]{1,3,2,0:T(8,128)S(1)} %fusion.85, bf16[64,16,1024]{2,0,1:T(8,128)(2,1)} %fusion.89, bf16[1024,256]{1,0:T(8,128)(2,1)S(1)} %bitcast.172, f32[64,16]{1,0:T(8,128)S(1)} %bitcast.180), kind=kOutput, calls=%fused_computation.27.clone.1 | convolution fusion | flops 268697600 | bytes 3440640 | tf_op jit(solution)/shard_map/while/body/eval_jaxpr/tgjk,gkd->tgjd/dot_general | solution.py:52
  94.6 2.8 %fusion.94 = bf16[8,64,16,128]{3,2,1,0:T(8,128)(2,1)} fusion(bf16[8,64,16,128]{3,2,1,0:T(8,128)(2,1)} %get-tuple-element.436, s32[]{:T(128)S(6)} %copy.80, f32[1,128,64,16]{1,3,2,0:T(8,128)} %fusion.90, bf16[64,16,576]{2,0,1:T(8,128)(2,1)S(1)} %fusion.93, f32[64,16]{1,0:T(8,128)S(1)} %bitcast.178, bf16[1024,256]{1,0:T(8,128)(2,1)} %get-tuple-element.466, ...), kind=kOutput, calls=%fused_computation.32.clone.1 | convolution fusion | flops 151388160 | bytes 2117644 | tf_op jit(solution)/shard_map/while/body/eval_jaxpr/tgjk,gkd->tgjd/dot_general | solution.py:52
  107.6 2.1 fusion.89
  109.8 3.7 %fusion.90 = f32[1,128,64,16]{1,3,2,0:T(8,128)} fusion(f32[1,128,64,16]{1,3,2,0:T(8,128)S(1)} %fusion.85, bf16[64,16,1024]{2,0,1:T(8,128)(2,1)} %fusion.89, bf16[1024,256]{1,0:T(8,128)(2,1)S(1)} %bitcast.172, f32[64,16]{1,0:T(8,128)S(1)} %bitcast.180), kind=kOutput, calls=%fused_computation.27.clone.1 | convolution fusion | flops 268697600 | bytes 3440640 | tf_op jit(solution)/shard_map/while/body/eval_jaxpr/tgjk,gkd->tgjd/dot_general | solution.py:52
  116.7 2.8 %fusion.94 = bf16[8,64,16,128]{3,2,1,0:T(8,128)(2,1)} fusion(bf16[8,64,16,128]{3,2,1,0:T(8,128)(2,1)} %get-tuple-element.436, s32[]{:T(128)S(6)} %copy.80, f32[1,128,64,16]{1,3,2,0:T(8,128)} %fusion.90, bf16[64,16,576]{2,0,1:T(8,128)(2,1)S(1)} %fusion.93, f32[64,16]{1,0:T(8,128)S(1)} %bitcast.178, bf16[1024,256]{1,0:T(8,128)(2,1)} %get-tuple-element.466, ...), kind=kOutput, calls=%fused_computation.32.clone.1 | convolution fusion | flops 151388160 | bytes 2117644 | tf_op jit(solution)/shard_map/while/body/eval_jaxpr/tgjk,gkd->tgjd/dot_general | solution.py:52
  129.7 2.1 fusion.89
  131.9 3.7 %fusion.90 = f32[1,128,64,16]{1,3,2,0:T(8,128)} fusion(f32[1,128,64,16]{1,3,2,0:T(8,128)S(1)} %fusion.85, bf16[64,16,1024]{2,0,1:T(8,128)(2,1)} %fusion.89, bf16[1024,256]{1,0:T(8,128)(2,1)S(1)} %bitcast.172, f32[64,16]{1,0:T(8,128)S(1)} %bitcast.180), kind=kOutput, calls=%fused_computation.27.clone.1 | convolution fusion | flops 268697600 | bytes 3440640 | tf_op jit(solution)/shard_map/while/body/eval_jaxpr/tgjk,gkd->tgjd/dot_general | solution.py:52
  138.9 2.8 %fusion.94 = bf16[8,64,16,128]{3,2,1,0:T(8,128)(2,1)} fusion(bf16[8,64,16,128]{3,2,1,0:T(8,128)(2,1)} %get-tuple-element.436, s32[]{:T(128)S(6)} %copy.80, f32[1,128,64,16]{1,3,2,0:T(8,128)} %fusion.90, bf16[64,16,576]{2,0,1:T(8,128)(2,1)S(1)} %fusion.93, f32[64,16]{1,0:T(8,128)S(1)} %bitcast.178, bf16[1024,256]{1,0:T(8,128)(2,1)} %get-tuple-element.466, ...), kind=kOutput, calls=%fused_computation.32.clone.1 | convolution fusion | flops 151388160 | bytes 2117644 | tf_op jit(solution)/shard_map/while/body/eval_jaxpr/tgjk,gkd->tgjd/dot_general | solution.py:52
  151.9 2.1 fusion.89
  154.0 3.7 %fusion.90 = f32[1,128,64,16]{1,3,2,0:T(8,128)} fusion(f32[1,128,64,16]{1,3,2,0:T(8,128)S(1)} %fusion.85, bf16[64,16,1024]{2,0,1:T(8,128)(2,1)} %fusion.89, bf16[1024,256]{1,0:T(8,128)(2,1)S(1)} %bitcast.172, f32[64,16]{1,0:T(8,128)S(1)} %bitcast.180), kind=kOutput, calls=%fused_computation.27.clone.1 | convolution fusion | flops 268697600 | bytes 3440640 | tf_op jit(solution)/shard_map/while/body/eval_jaxpr/tgjk,gkd->tgjd/dot_general | solution.py:52
  161.0 2.8 %fusion.94 = bf16[8,64,16,128]{3,2,1,0:T(8,128)(2,1)} fusion(bf16[8,64,16,128]{3,2,1,0:T(8,128)(2,1)} %get-tuple-element.436, s32[]{:T(128)S(6)} %copy.80, f32[1,128,64,16]{1,3,2,0:T(8,128)} %fusion.90, bf16[64,16,576]{2,0,1:T(8,128)(2,1)S(1)} %fusion.93, f32[64,16]{1,0:T(8,128)S(1)} %bitcast.178, bf16[1024,256]{1,0:T(8,128)(2,1)} %get-tuple-element.466, ...), kind=kOutput, calls=%fused_computation.32.clone.1 | convolution fusion | flops 151388160 | bytes 2117644 | tf_op jit(solution)/shard_map/while/body/eval_jaxpr/tgjk,gkd->tgjd/dot_general | solution.py:52
  174.0 2.1 fusion.89
  176.2 3.7 %fusion.90 = f32[1,128,64,16]{1,3,2,0:T(8,128)} fusion(f32[1,128,64,16]{1,3,2,0:T(8,128)S(1)} %fusion.85, bf16[64,16,1024]{2,0,1:T(8,128)(2,1)} %fusion.89, bf16[1024,256]{1,0:T(8,128)(2,1)S(1)} %bitcast.172, f32[64,16]{1,0:T(8,128)S(1)} %bitcast.180), kind=kOutput, calls=%fused_computation.27.clone.1 | convolution fusion | flops 268697600 | bytes 3440640 | tf_op jit(solution)/shard_map/while/body/eval_jaxpr/tgjk,gkd->tgjd/dot_general | solution.py:52
  183.1 2.8 %fusion.94 = bf16[8,64,16,128]{3,2,1,0:T(8,128)(2,1)} fusion(bf16[8,64,16,128]{3,2,1,0:T(8,128)(2,1)} %get-tuple-element.436, s32[]{:T(128)S(6)} %copy.80, f32[1,128,64,16]{1,3,2,0:T(8,128)} %fusion.90, bf16[64,16,576]{2,0,1:T(8,128)(2,1)S(1)} %fusion.93, f32[64,16]{1,0:T(8,128)S(1)} %bitcast.178, bf16[1024,256]{1,0:T(8,128)(2,1)} %get-tuple-element.466, ...), kind=kOutput, calls=%fused_computation.32.clone.1 | convolution fusion | flops 151388160 | bytes 2117644 | tf_op jit(solution)/shard_map/while/body/eval_jaxpr/tgjk,gkd->tgjd/dot_general | solution.py:52
  196.1 2.1 fusion.89
  198.3 3.7 %fusion.90 = f32[1,128,64,16]{1,3,2,0:T(8,128)} fusion(f32[1,128,64,16]{1,3,2,0:T(8,128)S(1)} %fusion.85, bf16[64,16,1024]{2,0,1:T(8,128)(2,1)} %fusion.89, bf16[1024,256]{1,0:T(8,128)(2,1)S(1)} %bitcast.172, f32[64,16]{1,0:T(8,128)S(1)} %bitcast.180), kind=kOutput, calls=%fused_computation.27.clone.1 | convolution fusion | flops 268697600 | bytes 3440640 | tf_op jit(solution)/shard_map/while/body/eval_jaxpr/tgjk,gkd->tgjd/dot_general | solution.py:52
  205.3 2.8 %fusion.94 = bf16[8,64,16,128]{3,2,1,0:T(8,128)(2,1)} fusion(bf16[8,64,16,128]{3,2,1,0:T(8,128)(2,1)} %get-tuple-element.436, s32[]{:T(128)S(6)} %copy.80, f32[1,128,64,16]{1,3,2,0:T(8,128)} %fusion.90, bf16[64,16,576]{2,0,1:T(8,128)(2,1)S(1)} %fusion.93, f32[64,16]{1,0:T(8,128)S(1)} %bitcast.178, bf16[1024,256]{1,0:T(8,128)(2,1)} %get-tuple-element.466, ...), kind=kOutput, calls=%fused_computation.32.clone.1 | convolution fusion | flops 151388160 | bytes 2117644 | tf_op jit(solution)/shard_map/while/body/eval_jaxpr/tgjk,gkd->tgjd/dot_general | solution.py:52
  218.3 2.1 fusion.89
  220.4 3.7 %fusion.90 = f32[1,128,64,16]{1,3,2,0:T(8,128)} fusion(f32[1,128,64,16]{1,3,2,0:T(8,128)S(1)} %fusion.85, bf16[64,16,1024]{2,0,1:T(8,128)(2,1)} %fusion.89, bf16[1024,256]{1,0:T(8,128)(2,1)S(1)} %bitcast.172, f32[64,16]{1,0:T(8,128)S(1)} %bitcast.180), kind=kOutput, calls=%fused_computation.27.clone.1 | convolution fusion | flops 268697600 | bytes 3440640 | tf_op jit(solution)/shard_map/while/body/eval_jaxpr/tgjk,gkd->tgjd/dot_general | solution.py:52
  227.4 2.8 %fusion.94 = bf16[8,64,16,128]{3,2,1,0:T(8,128)(2,1)} fusion(bf16[8,64,16,128]{3,2,1,0:T(8,128)(2,1)} %get-tuple-element.436, s32[]{:T(128)S(6)} %copy.80, f32[1,128,64,16]{1,3,2,0:T(8,128)} %fusion.90, bf16[64,16,576]{2,0,1:T(8,128)(2,1)S(1)} %fusion.93, f32[64,16]{1,0:T(8,128)S(1)} %bitcast.178, bf16[1024,256]{1,0:T(8,128)(2,1)} %get-tuple-element.466, ...), kind=kOutput, calls=%fused_computation.32.clone.1 | convolution fusion | flops 151388160 | bytes 2117644 | tf_op jit(solution)/shard_map/while/body/eval_jaxpr/tgjk,gkd->tgjd/dot_general | solution.py:52
  240.4 2.1 fusion.89
  242.6 3.7 %fusion.90 = f32[1,128,64,16]{1,3,2,0:T(8,128)} fusion(f32[1,128,64,16]{1,3,2,0:T(8,128)S(1)} %fusion.85, bf16[64,16,1024]{2,0,1:T(8,128)(2,1)} %fusion.89, bf16[1024,256]{1,0:T(8,128)(2,1)S(1)} %bitcast.172, f32[64,16]{1,0:T(8,128)S(1)} %bitcast.180), kind=kOutput, calls=%fused_computation.27.clone.1 | convolution fusion | flops 268697600 | bytes 3440640 | tf_op jit(solution)/shard_map/while/body/eval_jaxpr/tgjk,gkd->tgjd/dot_general | solution.py:52
  249.5 2.8 %fusion.94 = bf16[8,64,16,128]{3,2,1,0:T(8,128)(2,1)} fusion(bf16[8,64,16,128]{3,2,1,0:T(8,128)(2,1)} %get-tuple-element.436, s32[]{:T(128)S(6)} %copy.80, f32[1,128,64,16]{1,3,2,0:T(8,128)} %fusion.90, bf16[64,16,576]{2,0,1:T(8,128)(2,1)S(1)} %fusion.93, f32[64,16]{1,0:T(8,128)S(1)} %bitcast.178, bf16[1024,256]{1,0:T(8,128)(2,1)} %get-tuple-element.466, ...), kind=kOutput, calls=%fused_computation.32.clone.1 | convolution fusion | flops 151388160 | bytes 2117644 | tf_op jit(solution)/shard_map/while/body/eval_jaxpr/tgjk,gkd->tgjd/dot_general | solution.py:52
  (249 shorter events, 93.1 us)
Async XLA Ops:
  7.4 1.5 copy-start
  7.4 4.2 %copy-start.2 = (bf16[512,1,128]{2,0,1:T(8,128)(2,1)S(1)}, bf16[512,1,128]{2,0,1:T(8,128)(2,1)}, u32[]{:S(2)}) copy-start(bf16[512,1,128]{2,0,1:T(8,128)(2,1)} %param.13) | copy-start | bytes 393220
  7.4 4.2 %copy-start.3 = (bf16[512,1,128]{2,0,1:T(8,128)(2,1)S(1)}, bf16[512,1,128]{2,0,1:T(8,128)(2,1)}, u32[]{:S(2)}) copy-start(bf16[512,1,128]{2,0,1:T(8,128)(2,1)} %param.14) | copy-start | bytes 393220
  7.4 9.9 %copy-start.6 = (s32[8,1,16]{2,1,0:T(1,128)S(1)}, s32[8,1,16]{2,1,0:T(1,128)}, u32[]{:S(2)}) copy-start(s32[8,1,16]{2,1,0:T(1,128)} %param.17) | copy-start | bytes 1540
  7.4 10.0 %copy-start.4 = (f32[64,128]{1,0:T(8,128)S(1)}, f32[64,128]{1,0:T(8,128)}, u32[]{:S(2)}) copy-start(f32[64,128]{1,0:T(8,128)} %param.16) | copy-start | bytes 98308
  7.4 10.0 %copy-start.5 = (f32[64,128]{1,0:T(8,128)S(1)}, f32[64,128]{1,0:T(8,128)}, u32[]{:S(2)}) copy-start(f32[64,128]{1,0:T(8,128)} %param.15) | copy-start | bytes 98308
  7.4 43.8 %reduce-scatter.2.cloned.1.call-start = ((), (), s32[]{:S(2)}) async-start(), calls=%async_computation.1 | async-start | bytes 491520 | tf_op jit(solution)/shard_map/reduce_scatter | solution.py:74
  11.5 54.8 %all-gather.2.cloned.1.call-start = ((), (), s32[]{:S(2)}) async-start(), calls=%async_computation.2 | async-start | bytes 2359296 | tf_op jit(solution)/shard_map/all_gather | solution.py:88
  11.6 0.7 copy-start.1
  12.4 37.0 %collective-permute-start = (bf16[512,256]{1,0:T(8,128)(2,1)}, bf16[512,256]{1,0:T(8,128)(2,1)S(1)}, u32[]{:S(2)}, u32[]{:S(2)}) collective-permute-start(bf16[512,256]{1,0:T(8,128)(2,1)} %bitcast.175), channel_id=1, source_target_pairs={{0,4},{4,8},{8,12},{12,16},{16,20},{20,24},{24,28},{1,5},{5,9},{9,... | collective-permute-start | bytes 786440 | tf_op jit(solution)/shard_map/ppermute | solution.py:12
Sparse Core Ops, SparseCore 0:
  11.6 23.5 reduce-scatter.1
Sparse Core Ops, SparseCore 1:
  14.1 52.1 all-gather.1
where the time goes:
time: 262 us; the launch traced here: 260 us
  matrix products  84.4 us (32%)
  other arithmetic  51.1 us (20%)
  local copies, waits for them, and re-layouts  39.1 us (15%)
  blocking collectives  31 us (12%)
  loops' own time  20.8 us (8%)
  between operations  15 us (6%)
  waiting for transfers between devices  13.5 us (5%)
  starting transfers between devices  4.94 us (2%)
    dot_general x16, matrix products, attend(): jnp.einsum('tgjk,gkd->tgjd', rounded, value_rows, preferred_element_type=...  51.6 us
    all_gather x1, blocking collectives, body(): summaries = lax.all_gather(summary, 'ctx', axis=0, tiled=True)  31 us
    another operation x16, other arithmetic  21.9 us
    another operation x1, loops' own time, body(): results = lax.map(per_block, jnp.arange(blocks_here, dtype=jnp.int32))  20.8 us
    dot_general x16, matrix products, attend(): jnp.einsum('tgjd,gkd->tgjk', query_block_index, key_rows, preferred_eleme...  20 us
    reduce_sum x24, other arithmetic, attend(): total_w = jnp.sum(weights, axis=-1, keepdims=True)  17.6 us
    all_gather x1, waiting for transfers between devices, body(): all_blocks = lax.all_gather(blocks, 'ctx', axis=0, tiled=True)  13.4 us
    dynamic_slice x8, local copies, waits for them, and re-layouts, per_block(): lax.dynamic_index_in_dim(picked, block_num, 0, keepdims=False)  8.66 us
  transfers between devices with their start and end apart: 3, of which 1 were waited for; matrix products, arithmetic and copies ran while one was open for 2% of the time, Pallas kernels for 0%

commit v1 on v0

v1 whole, which is shorter than its diff:
```python
import functools

import jax
import jax.numpy as jnp
from jax import lax
from jax.experimental import pallas as pl
from jax.experimental.pallas import tpu as pltpu
from jax.sharding import PartitionSpec as P

WINDOW_TOKENS = 512
NEG = -1e30
LOG2E = 1.4426950408889634
F32 = jnp.float32
BF16 = jnp.bfloat16


def dot_t(a, b):
    return lax.dot_general(a, b, (((1,), (1,)), ((), ())), preferred_element_type=F32)


def attention_kernel(
    slot_ref, valid_ref, q_ref, kv_ref, win_ref, ck_ref, cv_ref, logit_ref, out_ref, k_sel, v_sel
):
    block = kv_ref.shape[1]
    width = q_ref.shape[2]
    heads = q_ref.shape[1]
    picked = slot_ref.shape[1]
    window = WINDOW_TOKENS
    num = pl.program_id(0)
    blocks_here = pl.num_programs(0)
    first_block = lax.axis_index("ctx") * blocks_here
    own_block = first_block + num
    factor = LOG2E * width**-0.5
    own_start = window + num * block
    own_rows = win_ref[pl.ds(own_start, block), :]
    k_sel[0:block, :] = own_rows[:, :width]
    v_sel[0:block, :width] = own_rows[:, width:]
    v_sel[0:block, width:] = jnp.ones((block, width), BF16)
    own_key = jnp.broadcast_to(own_rows[0:1, :width].astype(F32), (block, width))
    for k in range(1, picked):
        keep = valid_ref[num, k].astype(F32)
        rows = kv_ref[slot_ref[num, k]].astype(F32)
        at = slice(k * block, (k + 1) * block)
        k_sel[at, :] = (jnp.where(keep > 0, rows[:, :width], own_key)).astype(BF16)
        v_sel[at, :width] = jnp.where(keep > 0, rows[:, width:], 0.0).astype(BF16)
        v_sel[at, width:] = jnp.full((block, width), keep, F32).astype(BF16)
    k_win = win_ref[pl.ds(num * block, window + block), :width]
    v_win = win_ref[pl.ds(num * block, window + block), width:]
    v_win = jnp.concatenate([v_win, jnp.ones_like(v_win)], axis=1)
    tokens = 16
    rows_n = tokens * heads
    comp_n = ck_ref.shape[0]
    for c in range(block // tokens):
        q = q_ref[c * tokens : (c + 1) * tokens].reshape(rows_n, width)
        row = lax.broadcasted_iota(jnp.int32, (rows_n, 128), 0) // heads + c * tokens
        col = lax.broadcasted_iota(jnp.int32, (rows_n, 128), 1)
        gates = jax.nn.sigmoid(logit_ref[c * tokens : (c + 1) * tokens, :])
        gates = jnp.broadcast_to(gates[:, None, :], (tokens, heads, gates.shape[1])).reshape(
            rows_n, gates.shape[1]
        )
        head = lax.broadcasted_iota(jnp.int32, gates.shape, 0) % heads
        branch = lax.broadcasted_iota(jnp.int32, gates.shape, 1) - 3 * head
        gate = [
            jnp.sum(jnp.where(branch == b, gates, 0.0), axis=1, keepdims=True) for b in range(3)
        ]
        d = dot_t(q, k_sel[...])
        d = jnp.concatenate(
            [jnp.where((col <= row) | (col >= block), d[:, :128], NEG), d[:, 128:]], axis=1
        )
        m = jnp.max(d, axis=1, keepdims=True)
        p = jnp.exp2((d - m) * factor).astype(BF16)
        acc = jnp.dot(p, v_sel[...], preferred_element_type=F32)
        total = acc[:, :width] * (gate[1] / acc[:, width:])
        d = dot_t(q, k_win)
        low = window - first_block * block - num * block
        wcol = lax.broadcasted_iota(jnp.int32, (1, window - 128), 1) + 128
        head_part = jnp.where((col > row) & (col >= low), d[:, :128], NEG)
        mid_part = d[:, 128:window] + jnp.where(wcol >= low, 0.0, NEG)
        own_part = jnp.where(col[:, :block] <= row[:, :block], d[:, window:], NEG)
        d = jnp.concatenate([head_part, mid_part, own_part], axis=1)
        m = jnp.max(d, axis=1, keepdims=True)
        p = jnp.exp2((d - m) * factor).astype(BF16)
        acc = jnp.dot(p, v_win, preferred_element_type=F32)
        total += acc[:, :width] * (gate[2] / acc[:, width:])
        d = dot_t(jnp.concatenate([q, q], axis=1), ck_ref[...])
        crow = lax.broadcasted_iota(jnp.int32, (rows_n, comp_n), 0) // heads + c * tokens
        ccol = lax.broadcasted_iota(jnp.int32, (rows_n, comp_n), 1)
        d = jnp.where((ccol + 1) * block - 1 <= crow + own_block * block, d, NEG)
        m = jnp.maximum(jnp.max(d, axis=1, keepdims=True), 0.0)
        p = jnp.exp2((d - m) * factor)
        sums = jnp.sum(p, axis=1, keepdims=True) + jnp.exp2(-m * factor)
        acc = jnp.dot(p.astype(BF16), cv_ref[...], preferred_element_type=F32)
        total += (acc[:, :width] + acc[:, width:]) * (gate[0] / sums)
        out_ref[c * tokens : (c + 1) * tokens] = total.astype(BF16).reshape(tokens, heads, width)


def attention(slots, valid, queries, kv, win, ck, cv, logits, block):
    rows, heads, width = queries.shape
    blocks_here = rows // block
    picked = slots.shape[1]
    whole = pl.BlockSpec(memory_space=pltpu.VMEM)
    scalars = pl.BlockSpec(memory_space=pltpu.SMEM)
    return pl.pallas_call(
        attention_kernel,
        grid=(blocks_here,),
        out_shape=jax.ShapeDtypeStruct(queries.shape, BF16),
        in_specs=[
            scalars,
            scalars,
            pl.BlockSpec((block, heads, width), lambda i: (i, 0, 0)),
            whole,
            whole,
            whole,
            whole,
            pl.BlockSpec((block, logits.shape[1]), lambda i: (i, 0)),
        ],
        out_specs=pl.BlockSpec((block, heads, width), lambda i: (i, 0, 0)),
        scratch_shapes=[
            pltpu.VMEM((picked * block, width), BF16),
            pltpu.VMEM((picked * block, 2 * width), BF16),
        ],
        compiler_params=pltpu.CompilerParams(vmem_limit_bytes=48 * 1024 * 1024),
        cost_estimate=pl.CostEstimate(
            flops=7_000_000_000, bytes_accessed=8_000_000, transcendentals=14_000_000
        ),
    )(slots, valid, queries, kv, win, ck, cv, logits)


def split(value):
    high = value.astype(BF16)
    return jnp.concatenate([high, (value - high.astype(F32)).astype(BF16)], axis=1)


def body(
    hidden_in,
    gate_weight,
    encoded_queries,
    encoded_keys,
    value_tensor,
    comp_key_weight,
    comp_value_weight,
    selection,
):
    rows_here, heads_here, head_dim = encoded_queries.shape
    block_len = comp_key_weight.shape[0]
    blocks_here = rows_here // block_len
    own_index = lax.axis_index("ctx")
    count = lax.axis_size("ctx")
    partial_value = jnp.dot(hidden_in, gate_weight, preferred_element_type=F32)
    logits = lax.psum_scatter(partial_value, "head", scatter_dimension=1, tiled=True)
    key_value = jnp.concatenate([encoded_keys, value_tensor], axis=-1).reshape(
        rows_here, 2 * head_dim
    )
    previous = lax.ppermute(key_value, "ctx", [(s, s + 1) for s in range(count - 1)])
    extended = jnp.concatenate([previous, key_value], axis=0)
    all_blocks = lax.all_gather(
        key_value.reshape(blocks_here, block_len, 2 * head_dim), "ctx", axis=0, tiled=True
    )
    weights = jnp.concatenate([comp_key_weight, comp_value_weight], axis=-1)
    summaries = jnp.sum(all_blocks.astype(F32) * weights[None], axis=1)
    chosen = selection[:, 0, :]
    own_blocks = own_index * blocks_here + jnp.arange(blocks_here, dtype=jnp.int32)
    valid = (chosen <= own_blocks[:, None]).astype(jnp.int32)
    return attention(
        chosen,
        valid,
        encoded_queries,
        all_blocks,
        extended,
        split(summaries[:, :head_dim]),
        split(summaries[:, head_dim:]),
        logits,
        block_len,
    )


def solution(mesh):
    return jax.shard_map(
        body,
        mesh=mesh,
        in_specs=(
            P("ctx", "head"),
            P("head", None),
            P("ctx", "head", None),
            P("ctx", "head", None),
            P("ctx", "head", None),
            P(),
            P(),
            P("ctx", "head", None),
        ),
        out_specs=P("ctx", "head", None),
        check_vma=False,
    )
```

time: 262 us -> 110 us (0.42)
  matrix products: 84.4 us -> 2.59 us
  other arithmetic: 51.1 us -> 3.54 us
  local copies, waits for them, and re-layouts: 39.1 us -> 4.79 us
  waiting for transfers between devices: 13.5 us -> 46.8 us
  Pallas kernels: 0 us -> 32.2 us
  blocking collectives: 31 us -> 0 us
  loops' own time: 20.8 us -> 0 us
    dot_general x49 -> x0, matrix products: 84.4 us -> none  [the longest x16 51.6 us: attend(): jnp.einsum('tgjk,gkd->tgjd', rounded, value_rows, preferred_element_type=...]
    pallas_call x0 -> x1, Pallas kernels: none -> 32.2 us  [attention(): pl.pallas_call(attention_kernel, grid=(blocks_here,), out_shape=jax.Shape...]
    all_gather x1 -> x0, blocking collectives: 31 us -> none  [body(): summaries = lax.all_gather(summary, 'ctx', axis=0, tiled=True)]
    another operation x16 -> x0, other arithmetic: 21.9 us -> none
    dynamic_slice x24 -> x0, local copies, waits for them, and re-layouts: 21.2 us -> none  [the longest x8 8.66 us: per_block(): lax.dynamic_index_in_dim(picked, block_num, 0, keepdims=False)]
    another operation x1 -> x0, loops' own time: 20.8 us -> none  [body(): results = lax.map(per_block, jnp.arange(blocks_here, dtype=jnp.int32))]
    all_gather x1, waiting for transfers between devices: 13.4 us -> 29.9 us  [body(): lax.all_gather(key_value.reshape(blocks_here, block_len, 2 * head_dim), '...]
    reduce_sum x25 -> x1, other arithmetic: 18.6 us -> 2.44 us  [body(): summaries = jnp.sum(all_blocks.astype(F32) * weights[None], axis=1)]
  transfers between devices with their start and end apart: 3 -> 3, of which waited for: 1 -> 3; matrix products, arithmetic and copies ran while one was open for 2% -> 2% of each run, Pallas kernels for 0% -> 0%
where the time goes in v1:
time: 110 us
  waiting for transfers between devices  46.8 us (43%)
  Pallas kernels  32.2 us (29%)
  between operations  15 us (14%)
  starting transfers between devices  4.94 us (4%)
  local copies, waits for them, and re-layouts  4.79 us (4%)
  other arithmetic  3.54 us (3%)
  matrix products  2.59 us (2%)
    pallas_call x1, Pallas kernels, attention(): pl.pallas_call(attention_kernel, grid=(blocks_here,), out_shape=jax.Shape...  32.2 us
    all_gather x1, waiting for transfers between devices, body(): lax.all_gather(key_value.reshape(blocks_here, block_len, 2 * head_dim), '...  29.9 us
    unnamed x3, waiting for transfers between devices  11.2 us
    ppermute x1, waiting for transfers between devices, body(): lax.ppermute(key_value, 'ctx', [(s, s + 1) for s in range(count - 1)])  5.71 us
    ppermute x1, starting transfers between devices, body(): lax.ppermute(key_value, 'ctx', [(s, s + 1) for s in range(count - 1)])  4.86 us
    unnamed x20, local copies, waits for them, and re-layouts  4.76 us
    unnamed x1, matrix products  2.59 us
    reduce_sum x1, other arithmetic, body(): summaries = jnp.sum(all_blocks.astype(F32) * weights[None], axis=1)  2.44 us
  transfers between devices with their start and end apart: 3, of which 3 were waited for; matrix products, arithmetic and copies ran while one was open for 2% of the time, Pallas kernels for 0%

profile of v1, /device:TPU:0, one launch (start us, length us, event | category | flops | bytes accessed | tf_op | source)
XLA Modules:
  0.0 109.9 jit_solution(15157365455281023530)
XLA Ops:
  7.4 0.0 copy-start
  7.4 0.0 copy-start.5
  7.4 0.0 copy-start.6
  7.4 0.0 copy-start.7
  7.4 0.0 copy-start.8
  7.4 0.0 copy-start.2
  7.4 0.0 reduce-scatter.4.cloned.1.call-start
  7.4 1.4 %copy-done = bf16[512,1792]{1,0:T(8,128)(2,1)S(1)} copy-done((bf16[512,1792]{1,0:T(8,128)(2,1)S(1)}, bf16[512,1792]{1,0:T(8,128)(2,1)}, u32[]{:S(2)}) %copy-start) | copy-done | bytes 1835032
  8.9 2.6 %convolution_bitcast_fusion = f32[192,512]{1,0:T(8,128)} fusion(bf16[512,1792]{1,0:T(8,128)(2,1)S(1)} %copy-done, bf16[1792,192]{0,1:T(8,128)(2,1)} %param.9), kind=kOutput, calls=%fused_computation.1 | convolution fusion | flops 352321536 | bytes 2916352
  11.5 0.0 reduce-scatter.4.cloned.1.call-update
  11.5 0.0 all-gather.2.cloned.1.call-start
  11.5 0.0 copy-done.5
  11.6 0.0 copy-done.6
  11.6 0.0 copy-start.4
  11.6 0.7 copy-done.4
  12.3 0.0 all-gather.2.cloned.1.call-update
  12.3 4.9 %collective-permute-start = (bf16[512,256]{1,0:T(8,128)(2,1)}, bf16[512,256]{1,0:T(8,128)(2,1)S(1)}, u32[]{:S(2)}, u32[]{:S(2)}) collective-permute-start(bf16[512,256]{1,0:T(8,128)(2,1)} %bitcast.11), channel_id=1, source_target_pairs={{0,4},{4,8},{8,12},{12,16},{16,20},{20,24},{24,28},{1,5},{5,9},{9,... | collective-permute-start | bytes 786440 | tf_op jit(solution)/shard_map/ppermute | solution.py:154
  17.2 0.0 copy-done.7
  17.2 0.0 copy-done.8
  17.3 0.0 copy-done.2
  17.3 0.1 compare_convert_fusion.valid_ref
  17.3 5.7 %collective-permute-done = bf16[512,256]{1,0:T(8,128)(2,1)S(1)} collective-permute-done((bf16[512,256]{1,0:T(8,128)(2,1)}, bf16[512,256]{1,0:T(8,128)(2,1)S(1)}, u32[]{:S(2)}, u32[]{:S(2)}) %collective-permute-start) | collective-permute-done | bytes 262176 | tf_op jit(solution)/shard_map/ppermute | solution.py:154
  23.0 1.0 pad_maximum_fusion.win_ref
  24.0 11.1 %reduce-scatter.4.cloned.1.call-done = f32[48,512]{1,0:T(8,128)} async-done(((f32[192,512]{1,0:T(8,128)}), f32[48,512]{1,0:T(8,128)}) %reduce-scatter.4.cloned.1.call-update) | async-done | bytes 98320
  35.2 1.0 copy.13.logit_ref
  36.2 29.9 %all-gather.2.cloned.1.call-done.kv_ref = bf16[64,64,256]{2,1,0:T(8,128)(2,1)} async-done(((bf16[8,64,256]{2,1,0:T(8,128)(2,1)}), bf16[64,64,256]{2,1,0:T(8,128)(2,1)}) %all-gather.2.cloned.1.call-update) | async-done | bytes 2097168 | tf_op jit(solution)/shard_map/all_gather | solution.py:156
  66.1 0.0 copy-start.1
  66.1 2.4 %multiply_reduce_fusion = f32[64,256]{1,0:T(8,128)S(1)} fusion(bf16[64,64,256]{2,1,0:T(8,128)(2,1)} %all-gather.2.cloned.1.call-done.kv_ref, f32[64,256]{1,0:T(8,128)S(1)} %pad_maximum_fusion.1), kind=kLoop, calls=%fused_computation | loop fusion | flops 3129344 | bytes 2228224 | tf_op jit(solution)/shard_map/reduce_sum | solution.py:160
  68.6 0.0 copy-done.1
  68.6 0.0 copy-start.3
  68.7 1.6 %copy-done.3 = bf16[512,16,128]{2,1,0:T(8,128)(2,1)S(1)} copy-done((bf16[512,16,128]{2,1,0:T(8,128)(2,1)S(1)}, bf16[512,16,128]{2,1,0:T(8,128)(2,1)}, u32[]{:S(2)}) %copy-start.3) | copy-done | bytes 2097176
  70.2 32.2 %shard_map.82 = bf16[512,16,128]{2,1,0:T(8,128)(2,1)} custom-call(s32[8,16]{1,0:T(8,128)S(1)} %bitcast.9, s32[8,16]{1,0:T(8,128)S(1)} %compare_convert_fusion.valid_ref, bf16[512,16,128]{2,1,0:T(8,128)(2,1)S(1)} %copy-done.3, bf16[64,64,256]{2,1,0:T(8,128)(2,1)S(1)} %copy-done.1, bf16[1024,256]{1,0:T(8,128)(2,1)S(1)} %pad_maximum_fusion.win_ref, ...), custom_call_target="tpu_custom_call" | custom-call | flops 7000000000 | bytes 8000000 | tf_op jit(solution)/shard_map/pallas_call | solution.py:103
  (6 shorter events, 0.1 us)
Async XLA Ops:
  7.4 1.5 %copy-start = (bf16[512,1792]{1,0:T(8,128)(2,1)S(1)}, bf16[512,1792]{1,0:T(8,128)(2,1)}, u32[]{:S(2)}) copy-start(bf16[512,1792]{1,0:T(8,128)(2,1)} %param.8) | copy-start | bytes 5505028
  7.4 4.2 %copy-start.5 = (bf16[512,1,128]{2,0,1:T(8,128)(2,1)S(1)}, bf16[512,1,128]{2,0,1:T(8,128)(2,1)}, u32[]{:S(2)}) copy-start(bf16[512,1,128]{2,0,1:T(8,128)(2,1)} %param.11) | copy-start | bytes 393220
  7.4 4.2 %copy-start.6 = (bf16[512,1,128]{2,0,1:T(8,128)(2,1)S(1)}, bf16[512,1,128]{2,0,1:T(8,128)(2,1)}, u32[]{:S(2)}) copy-start(bf16[512,1,128]{2,0,1:T(8,128)(2,1)} %param.12) | copy-start | bytes 393220
  7.4 9.8 %copy-start.7 = (f32[64,128]{1,0:T(8,128)S(1)}, f32[64,128]{1,0:T(8,128)}, u32[]{:S(2)}) copy-start(f32[64,128]{1,0:T(8,128)} %param.14) | copy-start | bytes 98308
  7.4 9.8 %copy-start.8 = (f32[64,128]{1,0:T(8,128)S(1)}, f32[64,128]{1,0:T(8,128)}, u32[]{:S(2)}) copy-start(f32[64,128]{1,0:T(8,128)} %param.13) | copy-start | bytes 98308
  7.4 9.9 %copy-start.2 = (s32[8,1,16]{2,1,0:T(1,128)S(1)}, s32[8,1,16]{2,1,0:T(1,128)}, u32[]{:S(2)}) copy-start(s32[8,1,16]{2,1,0:T(1,128)} %param.15) | copy-start | bytes 1540
  7.4 27.8 %reduce-scatter.4.cloned.1.call-start = ((), (), s32[]{:S(2)}) async-start(), calls=%async_computation.2 | async-start | bytes 491520
  11.5 54.7 %all-gather.2.cloned.1.call-start = ((), (), s32[]{:S(2)}) async-start(), calls=%async_computation.1 | async-start | bytes 2359296 | tf_op jit(solution)/shard_map/all_gather | solution.py:156
  11.6 0.7 copy-start.4
  12.3 10.7 %collective-permute-start = (bf16[512,256]{1,0:T(8,128)(2,1)}, bf16[512,256]{1,0:T(8,128)(2,1)S(1)}, u32[]{:S(2)}, u32[]{:S(2)}) collective-permute-start(bf16[512,256]{1,0:T(8,128)(2,1)} %bitcast.11), channel_id=1, source_target_pairs={{0,4},{4,8},{8,12},{12,16},{16,20},{20,24},{24,28},{1,5},{5,9},{9,... | collective-permute-start | bytes 786440 | tf_op jit(solution)/shard_map/ppermute | solution.py:154
  66.1 2.5 %copy-start.1 = (bf16[64,64,256]{2,1,0:T(8,128)(2,1)S(1)}, bf16[64,64,256]{2,1,0:T(8,128)(2,1)}, u32[]{:S(2)}) copy-start(bf16[64,64,256]{2,1,0:T(8,128)(2,1)} %all-gather.2.cloned.1.call-done.kv_ref) | copy-start | bytes 6291460
  68.6 1.6 %copy-start.3 = (bf16[512,16,128]{2,1,0:T(8,128)(2,1)S(1)}, bf16[512,16,128]{2,1,0:T(8,128)(2,1)}, u32[]{:S(2)}) copy-start(bf16[512,16,128]{2,1,0:T(8,128)(2,1)} %q_ref.1) | copy-start | bytes 6291460
Sparse Core Ops, SparseCore 0:
  11.6 23.5 reduce-scatter.3
Sparse Core Ops, SparseCore 1:
  14.1 52.0 all-gather.1

commit v2 on v1

--- a/solution.py
+++ b/solution.py
@@ -18,36 +18,321 @@
     return lax.dot_general(a, b, (((1,), (1,)), ((), ())), preferred_element_type=F32)
 
 
+def split(value):
+    high = value.astype(BF16)
+    return jnp.concatenate([high, (value - high.astype(F32)).astype(BF16)], axis=1)
+
+
+SLOTS = 4
+MESH = pl.DeviceIdType.MESH
+
+
+def exchange_kernel(
+    hidden_ref,
+    weight_ref,
+    key_ref,
+    value_ref,
+    comp_ref,
+    sel_ref,
+    kv_ref,
+    sums_ref,
+    logit_ref,
+    slot_ref,
+    lists,
+    stage,
+    partial,
+    parts,
+    list_send,
+    list_recv,
+    data_send,
+    data_recv,
+    sums_send,
+    sums_recv,
+    part_send,
+    part_recv,
+    win_send,
+    win_recv,
+):
+    count = lax.axis_size("ctx")
+    head_count = lax.axis_size("head")
+    me = lax.axis_index("ctx")
+    my_head = lax.axis_index("head")
+    rows, width = key_ref.shape
+    block = comp_ref.shape[0]
+    blocks = rows // block
+    per = SLOTS * block
+    base = count * per
+    columns = logit_ref.shape[1]
+
+    barrier = pltpu.get_barrier_semaphore()
+
+    def greet(off, carry):
+        pl.semaphore_signal(
+            barrier, inc=1, device_id={"ctx": lax.rem(me + off, count)}, device_id_type=MESH
+        )
+        return carry
+
+    lax.fori_loop(1, count, greet, 0)
+    for off in range(1, head_count):
+        pl.semaphore_signal(
+            barrier,
+            inc=1,
+            device_id={"head": lax.rem(my_head + off, head_count)},
+            device_id_type=MESH,
+        )
+    kv_ref[pl.ds(base + rows, rows), :width] = key_ref[...]
+    kv_ref[pl.ds(base + rows, rows), width:] = value_ref[...]
+    summary = jnp.concatenate(
+        [
+            jnp.sum(
+                kv_ref[base + rows + n * block : base + rows + (n + 1) * block, :].astype(F32)
+                * comp_ref[...],
+                axis=0,
+                keepdims=True,
+            )
+            for n in range(blocks)
+        ],
+        axis=0,
+    )
+    sums_ref[me] = summary
+
+    @pl.when(me == 0)
+    def _():
+        kv_ref[base : base + rows, :] = jnp.zeros((rows, 2 * width), BF16)
+
+    def clear(j, carry):
+        sums_ref[j] = jnp.zeros(summary.shape, F32)
+        return carry
+
+    lax.fori_loop(me + 1, count, clear, 0)
+    pl.semaphore_wait(barrier, count - 1 + head_count - 1)
+
+    def list_copy(source, target):
+        return pltpu.make_async_remote_copy(
+            src_ref=sel_ref,
+            dst_ref=lists.at[source],
+            send_sem=list_send.at[target],
+            recv_sem=list_recv.at[source],
+            device_id={"ctx": target},
+            device_id_type=MESH,
+        )
+
+    def sums_copy(source, target):
+        return pltpu.make_async_remote_copy(
+            src_ref=sums_ref.at[source],
+            dst_ref=sums_ref.at[source],
+            send_sem=sums_send.at[target],
+            recv_sem=sums_recv.at[source],
+            device_id={"ctx": target},
+            device_id_type=MESH,
+        )
+
+    def data_copy(source, target):
+        return pltpu.make_async_remote_copy(
+            src_ref=stage.at[target],
+            dst_ref=kv_ref.at[pl.ds(pl.multiple_of(source * per, per), per)],
+            send_sem=data_send.at[target],
+            recv_sem=data_recv.at[source],
+            device_id={"ctx": target},
+            device_id_type=MESH,
+        )
+
+    def window_copy(target):
+        return pltpu.make_async_remote_copy(
+            src_ref=kv_ref.at[pl.ds(base + rows, rows)],
+            dst_ref=kv_ref.at[pl.ds(base, rows)],
+            send_sem=win_send,
+            recv_sem=win_recv,
+            device_id={"ctx": target},
+            device_id_type=MESH,
+        )
+
+    def part_copy(source, target):
+        return pltpu.make_async_remote_copy(
+            src_ref=partial.at[target],
+            dst_ref=parts.at[source],
+            send_sem=part_send.at[target],
+            recv_sem=part_recv.at[source],
+            device_id={"head": target},
+            device_id_type=MESH,
+        )
+
+    def each(first, last, step):
+        def run(j, carry):
+            step(j)
+            return carry
+
+        lax.fori_loop(first, last, run, 0)
+
+    each(0, me, lambda j: list_copy(me, j).start())
+
+    @pl.when(me < count - 1)
+    def _():
+        window_copy(me + 1).start()
+
+    each(me + 1, count, lambda j: sums_copy(me, j).start())
+
+    logits = jnp.dot(hidden_ref[...], weight_ref[...], preferred_element_type=F32).T
+    for h in range(head_count):
+        partial[h] = logits[h * columns : (h + 1) * columns, :]
+    for off in range(1, head_count):
+        part_copy(my_head, lax.rem(my_head + off, head_count)).start()
+
+    def pack(step, carry):
+        target = count - 1 - step
+        list_copy(target, me).wait_recv()
+        wanted = lists[target]
+        rank = jnp.zeros((1, 1), F32)
+        places = []
+        for n in range(blocks):
+            need = jnp.max(
+                jnp.where(wanted == me * blocks + n, 1.0, 0.0), axis=(0, 1), keepdims=True
+            )
+            places.append(jnp.where(need > 0, rank, -1.0))
+            rank = rank + need
+        for s in range(SLOTS):
+            packed = jnp.zeros((block, 2 * width), F32)
+            for n in range(blocks):
+                rows_n = kv_ref[base + rows + n * block : base + rows + (n + 1) * block, :]
+                packed = jnp.where(places[n] == s, rows_n.astype(F32), packed)
+            stage[target, s * block : (s + 1) * block, :] = packed.astype(BF16)
+        data_copy(me, target).start()
+        return carry
+
+    lax.fori_loop(0, count - 2 - me, pack, 0)
+
+    @pl.when(me < count - 1)
+    def _():
+        list_copy(me + 1, me).wait_recv()
+
+    mine = sel_ref[...]
+    query = lax.broadcasted_iota(jnp.int32, mine.shape, 0) + me * blocks
+
+    def place(j, slots):
+        rank = jnp.zeros((1, 1), F32)
+        for n in range(blocks):
+            named = mine == j * blocks + n
+            need = jnp.max(jnp.where(named, 1.0, 0.0), axis=(0, 1), keepdims=True)
+            packed = rank.astype(jnp.int32) + j * SLOTS
+            whole = count * SLOTS + n + (j - me + 1) * blocks
+            place_n = jnp.where(j < me - 1, packed, whole)
+            slots = jnp.where(named & (j * blocks + n <= query), place_n, slots)
+            rank = rank + need
+        return slots
+
+    slot_ref[...] = lax.fori_loop(0, me + 1, place, jnp.full(mine.shape, -1, jnp.int32))
+
+    for off in range(1, head_count):
+        part_copy(lax.rem(my_head + off, head_count), my_head).wait_recv()
+    total = partial[my_head]
+    for off in range(1, head_count):
+        total += parts[lax.rem(my_head + off, head_count)]
+    logit_ref[...] = total.T
+
+    each(0, me, lambda j: sums_copy(j, me).wait_recv())
+    each(0, me - 1, lambda j: data_copy(j, me).wait_recv())
+
+    @pl.when(me > 0)
+    def _():
+        window_copy(me).wait_recv()
+
+    each(0, me, lambda j: list_copy(me, j).wait_send())
+    each(me + 1, count, lambda j: sums_copy(me, j).wait_send())
+    each(me + 2, count, lambda j: data_copy(me, j).wait_send())
+
+    @pl.when(me < count - 1)
+    def _():
+        window_copy(me + 1).wait_send()
+
+    for off in range(1, head_count):
+        part_copy(my_head, lax.rem(my_head + off, head_count)).wait_send()
+
+
+def exchange(hidden, weight, keys, values, comp, lists, count, head_count):
+    rows, width = keys.shape
+    block = comp.shape[0]
+    blocks = rows // block
+    columns = weight.shape[1] // head_count
+    per = SLOTS * block
+    whole = pl.BlockSpec(memory_space=pltpu.VMEM)
+    dma = pltpu.SemaphoreType.DMA
+    return pl.pallas_call(
+        exchange_kernel,
+        out_shape=(
+            jax.ShapeDtypeStruct((count * per + 2 * rows, 2 * width), BF16),
+            jax.ShapeDtypeStruct((count, blocks, 2 * width), F32),
+            jax.ShapeDtypeStruct((rows, columns), F32),
+            jax.ShapeDtypeStruct(lists.shape, jnp.int32),
+        ),
+        in_specs=[whole] * 6,
+        out_specs=(whole,) * 4,
+        scratch_shapes=[
+            pltpu.VMEM((count,) + lists.shape, jnp.int32),
+            pltpu.VMEM((count, per, 2 * width), BF16),
+            pltpu.VMEM((head_count, columns, rows), F32),
+            pltpu.VMEM((head_count, columns, rows), F32),
+            dma((count,)),
+            dma((count,)),
+            dma((count,)),
+            dma((count,)),
+            dma((count,)),
+            dma((count,)),
+            dma((head_count,)),
+            dma((head_count,)),
+            dma,
+            dma,
+        ],
+        compiler_params=pltpu.CompilerParams(
+            collective_id=0, has_side_effects=True, vmem_limit_bytes=48 * 1024 * 1024
+        ),
+        cost_estimate=pl.CostEstimate(
+            flops=400_000_000, bytes_accessed=6_000_000, transcendentals=0
+        ),
+    )(hidden, weight, keys, values, comp, lists)
+
+
 def attention_kernel(
-    slot_ref, valid_ref, q_ref, kv_ref, win_ref, ck_ref, cv_ref, logit_ref, out_ref, k_sel, v_sel
+    slot_ref, q_ref, kv_ref, comp_ref, logit_ref, out_ref, k_sel, v_sel, ck_ref, cv_ref
 ):
-    block = kv_ref.shape[1]
+    block = q_ref.shape[0]
     width = q_ref.shape[2]
     heads = q_ref.shape[1]
-    picked = slot_ref.shape[1]
+    picked = k_sel.shape[0] // block
     window = WINDOW_TOKENS
     num = pl.program_id(0)
     blocks_here = pl.num_programs(0)
     first_block = lax.axis_index("ctx") * blocks_here
     own_block = first_block + num
     factor = LOG2E * width**-0.5
-    own_start = window + num * block
-    own_rows = win_ref[pl.ds(own_start, block), :]
+    shard = blocks_here * block
+    base = kv_ref.shape[0] - 2 * shard
+    own_start = pl.multiple_of(base + shard + num * block, block)
+    win_start = pl.multiple_of(own_start - window, block)
+
+    @pl.when(num == 0)
+    def _():
+        sums = comp_ref[...].reshape(ck_ref.shape)
+        ck_ref[...] = split(sums[:, :width])
+        cv_ref[...] = split(sums[:, width:])
+
+    own_rows = kv_ref[pl.ds(own_start, block), :]
     k_sel[0:block, :] = own_rows[:, :width]
     v_sel[0:block, :width] = own_rows[:, width:]
     v_sel[0:block, width:] = jnp.ones((block, width), BF16)
     own_key = jnp.broadcast_to(own_rows[0:1, :width].astype(F32), (block, width))
     for k in range(1, picked):
-        keep = valid_ref[num, k].astype(F32)
-        rows = kv_ref[slot_ref[num, k]].astype(F32)
+        slot = slot_ref[num, k]
+        keep = jnp.where(slot >= 0, 1.0, 0.0)
+        start = pl.multiple_of(jnp.maximum(slot, 0) * block, block)
+        rows = kv_ref[pl.ds(start, block), :].astype(F32)
         at = slice(k * block, (k + 1) * block)
         k_sel[at, :] = (jnp.where(keep > 0, rows[:, :width], own_key)).astype(BF16)
         v_sel[at, :width] = jnp.where(keep > 0, rows[:, width:], 0.0).astype(BF16)
         v_sel[at, width:] = jnp.full((block, width), keep, F32).astype(BF16)
-    k_win = win_ref[pl.ds(num * block, window + block), :width]
-    v_win = win_ref[pl.ds(num * block, window + block), width:]
+    k_win = kv_ref[pl.ds(win_start, window + block), :width]
+    v_win = kv_ref[pl.ds(win_start, window + block), width:]
     v_win = jnp.concatenate([v_win, jnp.ones_like(v_win)], axis=1)
-    tokens = 16
+    tokens = 32
     rows_n = tokens * heads
     comp_n = ck_ref.shape[0]
     for c in range(block // tokens):
@@ -94,10 +379,10 @@
         out_ref[c * tokens : (c + 1) * tokens] = total.astype(BF16).reshape(tokens, heads, width)
 
 
-def attention(slots, valid, queries, kv, win, ck, cv, logits, block):
+def attention(slots, queries, kv, sums, logits, block, picked):
     rows, heads, width = queries.shape
     blocks_here = rows // block
-    picked = slots.shape[1]
+    comp_n = sums.shape[0] * sums.shape[1]
     whole = pl.BlockSpec(memory_space=pltpu.VMEM)
     scalars = pl.BlockSpec(memory_space=pltpu.SMEM)
     return pl.pallas_call(
@@ -106,10 +391,7 @@
         out_shape=jax.ShapeDtypeStruct(queries.shape, BF16),
         in_specs=[
             scalars,
-            scalars,
             pl.BlockSpec((block, heads, width), lambda i: (i, 0, 0)),
-            whole,
-            whole,
             whole,
             whole,
             pl.BlockSpec((block, logits.shape[1]), lambda i: (i, 0)),
@@ -118,17 +400,14 @@
         scratch_shapes=[
             pltpu.VMEM((picked * block, width), BF16),
             pltpu.VMEM((picked * block, 2 * width), BF16),
+            pltpu.VMEM((comp_n, 2 * width), BF16),
+            pltpu.VMEM((comp_n, 2 * width), BF16),
         ],
         compiler_params=pltpu.CompilerParams(vmem_limit_bytes=48 * 1024 * 1024),
         cost_estimate=pl.CostEstimate(
             flops=7_000_000_000, bytes_accessed=8_000_000, transcendentals=14_000_000
         ),
-    )(slots, valid, queries, kv, win, ck, cv, logits)
-
-
-def split(value):
-    high = value.astype(BF16)
-    return jnp.concatenate([high, (value - high.astype(F32)).astype(BF16)], axis=1)
+    )(slots, queries, kv, sums, logits)
 
 
 def body(
@@ -143,35 +422,19 @@
 ):
     rows_here, heads_here, head_dim = encoded_queries.shape
     block_len = comp_key_weight.shape[0]
-    blocks_here = rows_here // block_len
-    own_index = lax.axis_index("ctx")
-    count = lax.axis_size("ctx")
-    partial_value = jnp.dot(hidden_in, gate_weight, preferred_element_type=F32)
-    logits = lax.psum_scatter(partial_value, "head", scatter_dimension=1, tiled=True)
-    key_value = jnp.concatenate([encoded_keys, value_tensor], axis=-1).reshape(
-        rows_here, 2 * head_dim
+    picked = selection.shape[-1]
+    lists = jnp.pad(selection[:, 0, :], ((0, 0), (0, 128 - picked)), constant_values=-1)
+    kv, sums, logits, slots = exchange(
+        hidden_in,
+        gate_weight,
+        encoded_keys.reshape(rows_here, head_dim),
+        value_tensor.reshape(rows_here, head_dim),
+        jnp.concatenate([comp_key_weight, comp_value_weight], axis=-1),
+        lists,
+        lax.axis_size("ctx"),
+        lax.axis_size("head"),
     )
-    previous = lax.ppermute(key_value, "ctx", [(s, s + 1) for s in range(count - 1)])
-    extended = jnp.concatenate([previous, key_value], axis=0)
-    all_blocks = lax.all_gather(
-        key_value.reshape(blocks_here, block_len, 2 * head_dim), "ctx", axis=0, tiled=True
-    )
-    weights = jnp.concatenate([comp_key_weight, comp_value_weight], axis=-1)
-    summaries = jnp.sum(all_blocks.astype(F32) * weights[None], axis=1)
-    chosen = selection[:, 0, :]
-    own_blocks = own_index * blocks_here + jnp.arange(blocks_here, dtype=jnp.int32)
-    valid = (chosen <= own_blocks[:, None]).astype(jnp.int32)
-    return attention(
-        chosen,
-        valid,
-        encoded_queries,
-        all_blocks,
-        extended,
-        split(summaries[:, :head_dim]),
-        split(summaries[:, head_dim:]),
-        logits,
-        block_len,
-    )
+    return attention(slots, encoded_queries, kv, sums, logits, block_len, picked)
 
 
 def solution(mesh):

time: 110 us -> 64.8 us (0.59)
  the two profiles are of different devices: /device:TPU:0 before, /device:TPU:24 now
where the time goes in v2:
time: 64.8 us; the launch traced here: 63.7 us
  Pallas kernels  57.5 us (89%)
  local copies, waits for them, and re-layouts  5.41 us (8%)
  other arithmetic  0.78 us (1%)
    pallas_call x1, Pallas kernels, exchange(): pl.pallas_call(exchange_kernel, out_shape=(jax.ShapeDtypeStruct((count *...  29.9 us
    pallas_call x1, Pallas kernels, attention(): pl.pallas_call(attention_kernel, grid=(blocks_here,), out_shape=jax.Shape...  27.6 us
    unnamed x9, local copies, waits for them, and re-layouts  4.72 us

profile of v2, /device:TPU:24, one launch (start us, length us, event | category | flops | bytes accessed | tf_op | source)
XLA Modules:
  0.0 63.7 jit_solution(15694730861901527265)
XLA Ops:
  0.0 0.7 %pad.4.sel_ref = s32[8,128]{1,0:T(8,128)S(1)} pad(s32[8,16]{1,0:T(8,128)} %bitcast.5, s32[]{:T(128)} %constant.0.clone.1), padding=0_0x0_112 | pad | bytes 4612 | tf_op jit(solution)/shard_map/jit(_pad)/pad | solution.py:426
  0.7 0.8 %pad_maximum_fusion.comp_ref = f32[64,256]{1,0:T(8,128)S(1)} fusion(f32[64,128]{1,0:T(8,128)} %param.14, f32[64,128]{1,0:T(8,128)} %param.13), kind=kLoop, calls=%fused_computation | loop fusion | flops 16384 | bytes 131072 | tf_op jit(solution)/shard_map/concatenate | solution.py:432
  1.5 1.4 %copy.9.weight_ref = bf16[1792,192]{1,0:T(8,128)(2,1)S(1)} copy(bf16[1792,192]{0,1:T(8,128)(2,1)} %param.9) | data formatting | bytes 1376256 | tf_op args[1]
  2.9 0.0 copy-start
  2.9 1.5 %copy-done = bf16[512,1792]{1,0:T(8,128)(2,1)S(1)} copy-done((bf16[512,1792]{1,0:T(8,128)(2,1)S(1)}, bf16[512,1792]{1,0:T(8,128)(2,1)}, u32[]{:S(2)}) %copy-start) | copy-done | bytes 1835032
  4.4 0.0 copy-start.1
  4.4 0.9 %copy-done.1 = bf16[512,1,128]{2,0,1:T(8,128)(2,1)S(1)} copy-done((bf16[512,1,128]{2,0,1:T(8,128)(2,1)S(1)}, bf16[512,1,128]{2,0,1:T(8,128)(2,1)}, u32[]{:S(2)}) %copy-start.1) | copy-done | bytes 131096
  5.3 0.0 copy-start.2
  5.3 0.9 %copy-done.2 = bf16[512,1,128]{2,0,1:T(8,128)(2,1)S(1)} copy-done((bf16[512,1,128]{2,0,1:T(8,128)(2,1)S(1)}, bf16[512,1,128]{2,0,1:T(8,128)(2,1)}, u32[]{:S(2)}) %copy-start.2) | copy-done | bytes 131096
  6.2 0.0 copy-start.3
  6.2 29.9 %shard_map.82 = (bf16[3072,256]{1,0:T(8,128)(2,1)S(1)}, f32[8,8,256]{2,1,0:T(8,128)S(1)}, f32[512,48]{1,0:T(8,128)S(1)}, s32[8,128]{1,0:T(8,128)S(1)}) custom-call(bf16[512,1792]{1,0:T(8,128)(2,1)S(1)} %copy-done, bf16[1792,192]{1,0:T(8,128)(2,1)S(1)} %copy.9.weight_ref, bf16[512,128]{1,0:T(8,128)(2,1)S(1)} %bitcast.3, bf16[512,128]{1,0:T(8,128)(2,1)S(1)} %bitcast.4, ...), custom_call_target="tpu_custom_call" | custom-call | flops 400000000 | bytes 6000000 | tf_op jit(solution)/shard_map/pallas_call | solution.py:259
  36.1 0.0 copy-done.3
  36.1 27.6 %shard_map.83 = bf16[512,16,128]{2,1,0:T(8,128)(2,1)} custom-call(s32[8,128]{1,0:T(8,128)S(1)} %get-tuple-element.9.slot_ref, bf16[512,16,128]{2,1,0:T(8,128)(2,1)S(1)} %copy-done.3, bf16[3072,256]{1,0:T(8,128)(2,1)S(1)} %get-tuple-element.10.kv_ref, f32[8,8,256]{2,1,0:T(8,128)S(1)} %get-tuple-element.11.comp_ref, f32[512,48]{1,0:T(8,128)S(1)} %get-tuple-element.12.logit_ref), custom_call_target="tpu_custom_call" | custom-call | flops 7000000000 | bytes 8000000 | tf_op jit(solution)/shard_map/pallas_call | solution.py:388
Async XLA Ops:
  2.9 1.5 %copy-start = (bf16[512,1792]{1,0:T(8,128)(2,1)S(1)}, bf16[512,1792]{1,0:T(8,128)(2,1)}, u32[]{:S(2)}) copy-start(bf16[512,1792]{1,0:T(8,128)(2,1)} %hidden_ref.1) | copy-start | bytes 5505028
  4.4 0.9 %copy-start.1 = (bf16[512,1,128]{2,0,1:T(8,128)(2,1)S(1)}, bf16[512,1,128]{2,0,1:T(8,128)(2,1)}, u32[]{:S(2)}) copy-start(bf16[512,1,128]{2,0,1:T(8,128)(2,1)} %param.11) | copy-start | bytes 393220
  5.3 0.9 %copy-start.2 = (bf16[512,1,128]{2,0,1:T(8,128)(2,1)S(1)}, bf16[512,1,128]{2,0,1:T(8,128)(2,1)}, u32[]{:S(2)}) copy-start(bf16[512,1,128]{2,0,1:T(8,128)(2,1)} %param.12) | copy-start | bytes 393220
  6.2 29.9 %copy-start.3 = (bf16[512,16,128]{2,1,0:T(8,128)(2,1)S(1)}, bf16[512,16,128]{2,1,0:T(8,128)(2,1)}, u32[]{:S(2)}) copy-start(bf16[512,16,128]{2,1,0:T(8,128)(2,1)} %q_ref.1) | copy-start | bytes 6291460

commit v3 on v2

--- a/solution.py
+++ b/solution.py
@@ -23,6 +23,47 @@
     return jnp.concatenate([high, (value - high.astype(F32)).astype(BF16)], axis=1)
 
 
+def token_gates(logits, heads, wanted):
+    tokens, columns = logits.shape
+    gates = jax.nn.sigmoid(logits)
+    gates = jnp.broadcast_to(gates[:, None, :], (tokens, heads, columns))
+    gates = gates.reshape(tokens * heads, columns)
+    head = lax.broadcasted_iota(jnp.int32, gates.shape, 0) % heads
+    branch = lax.broadcasted_iota(jnp.int32, gates.shape, 1) - 3 * head
+    return [
+        jnp.sum(jnp.where(branch == b, gates, 0.0), axis=1, keepdims=True) for b in wanted
+    ]
+
+
+def near_and_comp(q, gates, k_win, v_win, ck, cv, first_token, own_block, heads, block):
+    rows_n, width = q.shape
+    window = WINDOW_TOKENS
+    factor = LOG2E * width**-0.5
+    comp_n = ck.shape[0]
+    row = lax.broadcasted_iota(jnp.int32, (rows_n, 128), 0) // heads + first_token
+    col = lax.broadcasted_iota(jnp.int32, (rows_n, 128), 1)
+    d = dot_t(q, k_win)
+    low = window - own_block * block
+    wcol = lax.broadcasted_iota(jnp.int32, (1, window - 128), 1) + 128
+    head_part = jnp.where((col > row) & (col >= low), d[:, :128], NEG)
+    mid_part = d[:, 128:window] + jnp.where(wcol >= low, 0.0, NEG)
+    own_part = jnp.where(col[:, :block] <= row[:, :block], d[:, window:], NEG)
+    d = jnp.concatenate([head_part, mid_part, own_part], axis=1)
+    m = jnp.max(d, axis=1, keepdims=True)
+    p = jnp.exp2((d - m) * factor).astype(BF16)
+    acc = jnp.dot(p, v_win, preferred_element_type=F32)
+    total = acc[:, :width] * (gates[1] / acc[:, width:])
+    d = dot_t(jnp.concatenate([q, q], axis=1), ck)
+    crow = lax.broadcasted_iota(jnp.int32, (rows_n, comp_n), 0) // heads + first_token
+    ccol = lax.broadcasted_iota(jnp.int32, (rows_n, comp_n), 1)
+    d = jnp.where((ccol + 1) * block - 1 <= crow + own_block * block, d, NEG)
+    m = jnp.maximum(jnp.max(d, axis=1, keepdims=True), 0.0)
+    p = jnp.exp2((d - m) * factor)
+    sums = jnp.sum(p, axis=1, keepdims=True) + jnp.exp2(-m * factor)
+    acc = jnp.dot(p.astype(BF16), cv, preferred_element_type=F32)
+    return total + (acc[:, :width] + acc[:, width:]) * (gates[0] / sums)
+
+
 SLOTS = 4
 MESH = pl.DeviceIdType.MESH
 
@@ -32,12 +73,22 @@
     weight_ref,
     key_ref,
     value_ref,
-    comp_ref,
-    sel_ref,
+    comp_key_ref,
+    comp_value_ref,
+    short_ref,
+    query_ref,
     kv_ref,
-    sums_ref,
+    near_ref,
     logit_ref,
     slot_ref,
+    hidden,
+    queries,
+    keys,
+    values,
+    sel_ref,
+    sums_ref,
+    ck_ref,
+    cv_ref,
     lists,
     stage,
     partial,
@@ -52,18 +103,28 @@
     part_recv,
     win_send,
     win_recv,
+    load_sem,
 ):
     count = lax.axis_size("ctx")
     head_count = lax.axis_size("head")
     me = lax.axis_index("ctx")
     my_head = lax.axis_index("head")
     rows, width = key_ref.shape
-    block = comp_ref.shape[0]
+    block = comp_key_ref.shape[0]
+    heads = query_ref.shape[1]
     blocks = rows // block
     per = SLOTS * block
     base = count * per
     columns = logit_ref.shape[1]
 
+    loads = [
+        pltpu.make_async_copy(source, target, load_sem.at[n])
+        for n, (source, target) in enumerate(
+            ((key_ref, keys), (value_ref, values), (hidden_ref, hidden), (query_ref, queries))
+        )
+    ]
+    for load in loads:
+        load.start()
     barrier = pltpu.get_barrier_semaphore()
 
     def greet(off, carry):
@@ -80,13 +141,19 @@
             device_id={"head": lax.rem(my_head + off, head_count)},
             device_id_type=MESH,
         )
-    kv_ref[pl.ds(base + rows, rows), :width] = key_ref[...]
-    kv_ref[pl.ds(base + rows, rows), width:] = value_ref[...]
+    short = short_ref[...]
+    sel_ref[...] = jnp.full(sel_ref.shape, -1, jnp.int32)
+    sel_ref[:, : short.shape[1]] = short
+    loads[0].wait()
+    loads[1].wait()
+    kv_ref[pl.ds(base + rows, rows), :width] = keys[...]
+    kv_ref[pl.ds(base + rows, rows), width:] = values[...]
+    comp_weights = jnp.concatenate([comp_key_ref[...], comp_value_ref[...]], axis=1)
     summary = jnp.concatenate(
         [
             jnp.sum(
                 kv_ref[base + rows + n * block : base + rows + (n + 1) * block, :].astype(F32)
-                * comp_ref[...],
+                * comp_weights,
                 axis=0,
                 keepdims=True,
             )
@@ -172,7 +239,8 @@
 
     each(me + 1, count, lambda j: sums_copy(me, j).start())
 
-    logits = jnp.dot(hidden_ref[...], weight_ref[...], preferred_element_type=F32).T
+    loads[2].wait()
+    logits = dot_t(weight_ref[...], hidden[...])
     for h in range(head_count):
         partial[h] = logits[h * columns : (h + 1) * columns, :]
     for off in range(1, head_count):
@@ -230,12 +298,41 @@
     logit_ref[...] = total.T
 
     each(0, me, lambda j: sums_copy(j, me).wait_recv())
-    each(0, me - 1, lambda j: data_copy(j, me).wait_recv())
 
     @pl.when(me > 0)
     def _():
         window_copy(me).wait_recv()
 
+    sums = sums_ref[...].reshape(ck_ref.shape)
+    ck_ref[...] = split(sums[:, :width])
+    cv_ref[...] = split(sums[:, width:])
+    loads[3].wait()
+    tokens = 32
+
+    def near(n, carry):
+        start = base + rows + n * block - WINDOW_TOKENS
+        k_win = kv_ref[pl.ds(pl.multiple_of(start, block), WINDOW_TOKENS + block), :width]
+        v_win = kv_ref[pl.ds(pl.multiple_of(start, block), WINDOW_TOKENS + block), width:]
+        v_win = jnp.concatenate([v_win, jnp.ones_like(v_win)], axis=1)
+        for c in range(block // tokens):
+            at = pl.ds(pl.multiple_of(n * block + c * tokens, tokens), tokens)
+            result = near_and_comp(
+                queries[at].reshape(tokens * heads, width),
+                token_gates(logit_ref[at, :], heads, (0, 2)),
+                k_win,
+                v_win,
+                ck_ref[...],
+                cv_ref[...],
+                c * tokens,
+                me * blocks + n,
+                heads,
+                block,
+            )
+            near_ref[at] = result.reshape(tokens, heads, width)
+        return carry
+
+    lax.fori_loop(0, blocks, near, 0)
+    each(0, me - 1, lambda j: data_copy(j, me).wait_recv())
     each(0, me, lambda j: list_copy(me, j).wait_send())
     each(me + 1, count, lambda j: sums_copy(me, j).wait_send())
     each(me + 2, count, lambda j: data_copy(me, j).wait_send())
@@ -248,26 +345,36 @@
         part_copy(my_head, lax.rem(my_head + off, head_count)).wait_send()
 
 
-def exchange(hidden, weight, keys, values, comp, lists, count, head_count):
+def exchange(hidden, weight, keys, values, comp_key, comp_value, lists, queries, count, head_count):
     rows, width = keys.shape
-    block = comp.shape[0]
+    block = comp_key.shape[0]
     blocks = rows // block
-    columns = weight.shape[1] // head_count
+    columns = weight.shape[0] // head_count
+    padded = (blocks, 128)
     per = SLOTS * block
     whole = pl.BlockSpec(memory_space=pltpu.VMEM)
+    far = pl.BlockSpec(memory_space=pltpu.HBM)
     dma = pltpu.SemaphoreType.DMA
     return pl.pallas_call(
         exchange_kernel,
         out_shape=(
             jax.ShapeDtypeStruct((count * per + 2 * rows, 2 * width), BF16),
-            jax.ShapeDtypeStruct((count, blocks, 2 * width), F32),
+            jax.ShapeDtypeStruct(queries.shape, F32),
             jax.ShapeDtypeStruct((rows, columns), F32),
-            jax.ShapeDtypeStruct(lists.shape, jnp.int32),
+            jax.ShapeDtypeStruct(padded, jnp.int32),
         ),
-        in_specs=[whole] * 6,
+        in_specs=[far, whole, far, far, whole, whole, whole, far],
         out_specs=(whole,) * 4,
         scratch_shapes=[
-            pltpu.VMEM((count,) + lists.shape, jnp.int32),
+            pltpu.VMEM(hidden.shape, BF16),
+            pltpu.VMEM(queries.shape, BF16),
+            pltpu.VMEM(keys.shape, BF16),
+            pltpu.VMEM(values.shape, BF16),
+            pltpu.VMEM(padded, jnp.int32),
+            pltpu.VMEM((count, blocks, 2 * width), F32),
+            pltpu.VMEM((count * blocks, 2 * width), BF16),
+            pltpu.VMEM((count * blocks, 2 * width), BF16),
+            pltpu.VMEM((count,) + padded, jnp.int32),
             pltpu.VMEM((count, per, 2 * width), BF16),
             pltpu.VMEM((head_count, columns, rows), F32),
             pltpu.VMEM((head_count, columns, rows), F32),
@@ -281,40 +388,24 @@
             dma((head_count,)),
             dma,
             dma,
+            dma((4,)),
         ],
         compiler_params=pltpu.CompilerParams(
             collective_id=0, has_side_effects=True, vmem_limit_bytes=48 * 1024 * 1024
         ),
         cost_estimate=pl.CostEstimate(
-            flops=400_000_000, bytes_accessed=6_000_000, transcendentals=0
+            flops=3_000_000_000, bytes_accessed=6_000_000, transcendentals=5_000_000
         ),
-    )(hidden, weight, keys, values, comp, lists)
-
-
-def attention_kernel(
-    slot_ref, q_ref, kv_ref, comp_ref, logit_ref, out_ref, k_sel, v_sel, ck_ref, cv_ref
-):
-    block = q_ref.shape[0]
-    width = q_ref.shape[2]
-    heads = q_ref.shape[1]
+    )(hidden, weight, keys, values, comp_key, comp_value, lists, queries)
+
+
+def selected_kernel(slot_ref, q_ref, kv_ref, near_ref, logit_ref, out_ref, k_sel, v_sel):
+    block, heads, width = q_ref.shape
     picked = k_sel.shape[0] // block
-    window = WINDOW_TOKENS
     num = pl.program_id(0)
-    blocks_here = pl.num_programs(0)
-    first_block = lax.axis_index("ctx") * blocks_here
-    own_block = first_block + num
     factor = LOG2E * width**-0.5
-    shard = blocks_here * block
-    base = kv_ref.shape[0] - 2 * shard
-    own_start = pl.multiple_of(base + shard + num * block, block)
-    win_start = pl.multiple_of(own_start - window, block)
-
-    @pl.when(num == 0)
-    def _():
-        sums = comp_ref[...].reshape(ck_ref.shape)
-        ck_ref[...] = split(sums[:, :width])
-        cv_ref[...] = split(sums[:, width:])
-
+    shard = pl.num_programs(0) * block
+    own_start = pl.multiple_of(kv_ref.shape[0] - shard + num * block, block)
     own_rows = kv_ref[pl.ds(own_start, block), :]
     k_sel[0:block, :] = own_rows[:, :width]
     v_sel[0:block, :width] = own_rows[:, width:]
@@ -329,25 +420,14 @@
         k_sel[at, :] = (jnp.where(keep > 0, rows[:, :width], own_key)).astype(BF16)
         v_sel[at, :width] = jnp.where(keep > 0, rows[:, width:], 0.0).astype(BF16)
         v_sel[at, width:] = jnp.full((block, width), keep, F32).astype(BF16)
-    k_win = kv_ref[pl.ds(win_start, window + block), :width]
-    v_win = kv_ref[pl.ds(win_start, window + block), width:]
-    v_win = jnp.concatenate([v_win, jnp.ones_like(v_win)], axis=1)
-    tokens = 32
+    tokens = 64
     rows_n = tokens * heads
-    comp_n = ck_ref.shape[0]
     for c in range(block // tokens):
-        q = q_ref[c * tokens : (c + 1) * tokens].reshape(rows_n, width)
+        at = slice(c * tokens, (c + 1) * tokens)
+        q = q_ref[at].reshape(rows_n, width)
         row = lax.broadcasted_iota(jnp.int32, (rows_n, 128), 0) // heads + c * tokens
         col = lax.broadcasted_iota(jnp.int32, (rows_n, 128), 1)
-        gates = jax.nn.sigmoid(logit_ref[c * tokens : (c + 1) * tokens, :])
-        gates = jnp.broadcast_to(gates[:, None, :], (tokens, heads, gates.shape[1])).reshape(
-            rows_n, gates.shape[1]
-        )
-        head = lax.broadcasted_iota(jnp.int32, gates.shape, 0) % heads
-        branch = lax.broadcasted_iota(jnp.int32, gates.shape, 1) - 3 * head
-        gate = [
-            jnp.sum(jnp.where(branch == b, gates, 0.0), axis=1, keepdims=True) for b in range(3)
-        ]
+        gate = token_gates(logit_ref[at, :], heads, (1,))[0]
         d = dot_t(q, k_sel[...])
         d = jnp.concatenate(
             [jnp.where((col <= row) | (col >= block), d[:, :128], NEG), d[:, 128:]], axis=1
@@ -355,59 +435,36 @@
         m = jnp.max(d, axis=1, keepdims=True)
         p = jnp.exp2((d - m) * factor).astype(BF16)
         acc = jnp.dot(p, v_sel[...], preferred_element_type=F32)
-        total = acc[:, :width] * (gate[1] / acc[:, width:])
-        d = dot_t(q, k_win)
-        low = window - first_block * block - num * block
-        wcol = lax.broadcasted_iota(jnp.int32, (1, window - 128), 1) + 128
-        head_part = jnp.where((col > row) & (col >= low), d[:, :128], NEG)
-        mid_part = d[:, 128:window] + jnp.where(wcol >= low, 0.0, NEG)
-        own_part = jnp.where(col[:, :block] <= row[:, :block], d[:, window:], NEG)
-        d = jnp.concatenate([head_part, mid_part, own_part], axis=1)
-        m = jnp.max(d, axis=1, keepdims=True)
-        p = jnp.exp2((d - m) * factor).astype(BF16)
-        acc = jnp.dot(p, v_win, preferred_element_type=F32)
-        total += acc[:, :width] * (gate[2] / acc[:, width:])
-        d = dot_t(jnp.concatenate([q, q], axis=1), ck_ref[...])
-        crow = lax.broadcasted_iota(jnp.int32, (rows_n, comp_n), 0) // heads + c * tokens
-        ccol = lax.broadcasted_iota(jnp.int32, (rows_n, comp_n), 1)
-        d = jnp.where((ccol + 1) * block - 1 <= crow + own_block * block, d, NEG)
-        m = jnp.maximum(jnp.max(d, axis=1, keepdims=True), 0.0)
-        p = jnp.exp2((d - m) * factor)
-        sums = jnp.sum(p, axis=1, keepdims=True) + jnp.exp2(-m * factor)
-        acc = jnp.dot(p.astype(BF16), cv_ref[...], preferred_element_type=F32)
-        total += (acc[:, :width] + acc[:, width:]) * (gate[0] / sums)
-        out_ref[c * tokens : (c + 1) * tokens] = total.astype(BF16).reshape(tokens, heads, width)
-
-
-def attention(slots, queries, kv, sums, logits, block, picked):
+        total = near_ref[at].reshape(rows_n, width) + acc[:, :width] * (gate / acc[:, width:])
+        out_ref[at] = total.astype(BF16).reshape(tokens, heads, width)
+
+
+def selected(slots, queries, kv, near, logits, block, picked):
     rows, heads, width = queries.shape
     blocks_here = rows // block
-    comp_n = sums.shape[0] * sums.shape[1]
     whole = pl.BlockSpec(memory_space=pltpu.VMEM)
     scalars = pl.BlockSpec(memory_space=pltpu.SMEM)
     return pl.pallas_call(
-        attention_kernel,
+        selected_kernel,
         grid=(blocks_here,),
         out_shape=jax.ShapeDtypeStruct(queries.shape, BF16),
         in_specs=[
             scalars,
             pl.BlockSpec((block, heads, width), lambda i: (i, 0, 0)),
             whole,
-            whole,
+            pl.BlockSpec((block, heads, width), lambda i: (i, 0, 0)),
             pl.BlockSpec((block, logits.shape[1]), lambda i: (i, 0)),
         ],
         out_specs=pl.BlockSpec((block, heads, width), lambda i: (i, 0, 0)),
         scratch_shapes=[
             pltpu.VMEM((picked * block, width), BF16),
             pltpu.VMEM((picked * block, 2 * width), BF16),
-            pltpu.VMEM((comp_n, 2 * width), BF16),
-            pltpu.VMEM((comp_n, 2 * width), BF16),
         ],
         compiler_params=pltpu.CompilerParams(vmem_limit_bytes=48 * 1024 * 1024),
         cost_estimate=pl.CostEstimate(
-            flops=7_000_000_000, bytes_accessed=8_000_000, transcendentals=14_000_000
+            flops=4_500_000_000, bytes_accessed=8_000_000, transcendentals=9_000_000
         ),
-    )(slots, queries, kv, sums, logits)
+    )(slots, queries, kv, near, logits)
 
 
 def body(
@@ -423,18 +480,19 @@
     rows_here, heads_here, head_dim = encoded_queries.shape
     block_len = comp_key_weight.shape[0]
     picked = selection.shape[-1]
-    lists = jnp.pad(selection[:, 0, :], ((0, 0), (0, 128 - picked)), constant_values=-1)
-    kv, sums, logits, slots = exchange(
+    kv, near, logits, slots = exchange(
         hidden_in,
-        gate_weight,
+        gate_weight.T,
         encoded_keys.reshape(rows_here, head_dim),
         value_tensor.reshape(rows_here, head_dim),
-        jnp.concatenate([comp_key_weight, comp_value_weight], axis=-1),
-        lists,
+        comp_key_weight,
+        comp_value_weight,
+        selection[:, 0, :],
+        encoded_queries,
         lax.axis_size("ctx"),
         lax.axis_size("head"),
     )
-    return attention(slots, encoded_queries, kv, sums, logits, block_len, picked)
+    return selected(slots, encoded_queries, kv, near, logits, block_len, picked)
 
 
 def solution(mesh):

time: 64.8 us -> 67.7 us (1.045); the launches traced: 63.7 us -> 67.3 us
  Pallas kernels: 57.5 us -> 60.7 us
  local copies, waits for them, and re-layouts: 5.41 us -> 6.61 us
  other arithmetic: 0.78 us -> 0 us
    pallas_call x1, Pallas kernels: 29.9 us -> 39.4 us  [exchange(): pl.pallas_call(exchange_kernel, out_shape=(jax.ShapeDtypeStruct((count *...]
    pallas_call x1, Pallas kernels: 27.6 us -> 21.3 us  [selected(): pl.pallas_call(selected_kernel, grid=(blocks_here,), out_shape=jax.ShapeD...]
    unnamed x9 -> x16, local copies, waits for them, and re-layouts: 4.72 us -> 6.61 us
    concatenate x1 -> x0, other arithmetic: 0.78 us -> none  [body(): jnp.concatenate([comp_key_weight, comp_value_weight], axis=-1)]
    pad x1 -> x0, local copies, waits for them, and re-layouts: 0.69 us -> none  [body(): jnp.pad(selection[:, 0, :], ((0, 0), (0, 128 - picked)), constant_values=-1)]
where the time goes in v3:
time: 67.7 us; the launch traced here: 67.3 us
  Pallas kernels  60.7 us (90%)
  local copies, waits for them, and re-layouts  6.61 us (10%)
    pallas_call x1, Pallas kernels, exchange(): pl.pallas_call(exchange_kernel, out_shape=(jax.ShapeDtypeStruct((count *...  39.4 us
    pallas_call x1, Pallas kernels, selected(): pl.pallas_call(selected_kernel, grid=(blocks_here,), out_shape=jax.ShapeD...  21.3 us
    unnamed x16, local copies, waits for them, and re-layouts  6.61 us

profile of v3, /device:TPU:24, one launch (start us, length us, event | category | flops | bytes accessed | tf_op | source)
XLA Modules:
  0.0 67.3 jit_solution(15048295021447256228)
XLA Ops:
  0.0 0.0 copy-start.1
  0.0 1.5 %copy-done.1 = bf16[512,1792]{1,0:T(8,128)(2,1)S(1)} copy-done((bf16[512,1792]{1,0:T(8,128)(2,1)S(1)}, bf16[512,1792]{1,0:T(8,128)(2,1)}, u32[]{:S(2)}) %copy-start.1) | copy-done | bytes 1835032
  1.5 0.0 copy-start.2
  1.5 1.1 %copy-done.2 = bf16[1792,192]{0,1:T(8,128)(2,1)S(1)} copy-done((bf16[1792,192]{0,1:T(8,128)(2,1)S(1)}, bf16[1792,192]{0,1:T(8,128)(2,1)}, u32[]{:S(2)}) %copy-start.2) | copy-done | bytes 688152
  2.6 0.0 copy-start.3
  2.6 0.9 %copy-done.3 = bf16[512,1,128]{2,0,1:T(8,128)(2,1)S(1)} copy-done((bf16[512,1,128]{2,0,1:T(8,128)(2,1)S(1)}, bf16[512,1,128]{2,0,1:T(8,128)(2,1)}, u32[]{:S(2)}) %copy-start.3) | copy-done | bytes 131096
  3.5 0.0 copy-start.4
  3.5 0.9 %copy-done.4 = bf16[512,1,128]{2,0,1:T(8,128)(2,1)S(1)} copy-done((bf16[512,1,128]{2,0,1:T(8,128)(2,1)S(1)}, bf16[512,1,128]{2,0,1:T(8,128)(2,1)}, u32[]{:S(2)}) %copy-start.4) | copy-done | bytes 131096
  4.4 0.0 copy-start.5
  4.4 0.8 %copy-done.5 = f32[64,128]{1,0:T(8,128)S(1)} copy-done((f32[64,128]{1,0:T(8,128)S(1)}, f32[64,128]{1,0:T(8,128)}, u32[]{:S(2)}) %copy-start.5) | copy-done | bytes 32792
  5.2 0.0 copy-start.6
  5.2 0.8 %copy-done.6 = f32[64,128]{1,0:T(8,128)S(1)} copy-done((f32[64,128]{1,0:T(8,128)S(1)}, f32[64,128]{1,0:T(8,128)}, u32[]{:S(2)}) %copy-start.6) | copy-done | bytes 32792
  5.9 0.0 copy-start.7
  5.9 0.7 %copy-done.7 = s32[8,1,16]{2,1,0:T(1,128)S(1)} copy-done((s32[8,1,16]{2,1,0:T(1,128)S(1)}, s32[8,1,16]{2,1,0:T(1,128)}, u32[]{:S(2)}) %copy-start.7) | copy-done | bytes 536
  6.6 0.0 copy-start
  6.6 39.4 %shard_map.82 = (bf16[3072,256]{1,0:T(8,128)(2,1)S(1)}, f32[512,16,128]{2,1,0:T(8,128)}, f32[512,48]{1,0:T(8,128)S(1)}, s32[8,128]{1,0:T(8,128)S(1)}) custom-call(bf16[512,1792]{1,0:T(8,128)(2,1)S(1)} %copy-done.1, bf16[192,1792]{1,0:T(8,128)(2,1)S(1)} %bitcast.4, bf16[512,128]{1,0:T(8,128)(2,1)S(1)} %bitcast.5, bf16[512,128]{1,0:T(8,128)(2,1)S(1)} %bitcast.6, ...), custom_call_target="tpu_custom_call" | custom-call | flops 3000000000 | bytes 6000000 | tf_op jit(solution)/shard_map/pallas_call | solution.py:358
  46.0 0.0 copy-done
  46.0 21.3 %shard_map.83 = bf16[512,16,128]{2,1,0:T(8,128)(2,1)} custom-call(s32[8,128]{1,0:T(8,128)S(1)} %get-tuple-element.9.slot_ref, bf16[512,16,128]{2,1,0:T(8,128)(2,1)S(1)} %copy-done, bf16[3072,256]{1,0:T(8,128)(2,1)S(1)} %get-tuple-element.10.kv_ref, f32[512,16,128]{2,1,0:T(8,128)} %get-tuple-element.11.near_ref, f32[512,48]{1,0:T(8,128)S(1)} %get-tuple-element.12.logit_ref), custom_call_target="tpu_custom_call" | custom-call | flops 4499999744 | bytes 8000000 | tf_op jit(solution)/shard_map/pallas_call | solution.py:447
Async XLA Ops:
  0.0 1.5 %copy-start.1 = (bf16[512,1792]{1,0:T(8,128)(2,1)S(1)}, bf16[512,1792]{1,0:T(8,128)(2,1)}, u32[]{:S(2)}) copy-start(bf16[512,1792]{1,0:T(8,128)(2,1)} %hidden_ref.1) | copy-start | bytes 5505028
  1.5 1.1 %copy-start.2 = (bf16[1792,192]{0,1:T(8,128)(2,1)S(1)}, bf16[1792,192]{0,1:T(8,128)(2,1)}, u32[]{:S(2)}) copy-start(bf16[1792,192]{0,1:T(8,128)(2,1)} %param.9) | copy-start | bytes 2064388
  2.6 0.9 %copy-start.3 = (bf16[512,1,128]{2,0,1:T(8,128)(2,1)S(1)}, bf16[512,1,128]{2,0,1:T(8,128)(2,1)}, u32[]{:S(2)}) copy-start(bf16[512,1,128]{2,0,1:T(8,128)(2,1)} %param.11) | copy-start | bytes 393220
  3.5 0.9 %copy-start.4 = (bf16[512,1,128]{2,0,1:T(8,128)(2,1)S(1)}, bf16[512,1,128]{2,0,1:T(8,128)(2,1)}, u32[]{:S(2)}) copy-start(bf16[512,1,128]{2,0,1:T(8,128)(2,1)} %param.12) | copy-start | bytes 393220
  4.4 0.8 %copy-start.5 = (f32[64,128]{1,0:T(8,128)S(1)}, f32[64,128]{1,0:T(8,128)}, u32[]{:S(2)}) copy-start(f32[64,128]{1,0:T(8,128)} %comp_key_ref.1) | copy-start | bytes 98308
  5.2 0.8 %copy-start.6 = (f32[64,128]{1,0:T(8,128)S(1)}, f32[64,128]{1,0:T(8,128)}, u32[]{:S(2)}) copy-start(f32[64,128]{1,0:T(8,128)} %comp_value_ref.1) | copy-start | bytes 98308
  5.9 0.7 %copy-start.7 = (s32[8,1,16]{2,1,0:T(1,128)S(1)}, s32[8,1,16]{2,1,0:T(1,128)}, u32[]{:S(2)}) copy-start(s32[8,1,16]{2,1,0:T(1,128)} %param.15) | copy-start | bytes 1540
  6.6 39.4 %copy-start = (bf16[512,16,128]{2,1,0:T(8,128)(2,1)S(1)}, bf16[512,16,128]{2,1,0:T(8,128)(2,1)}, u32[]{:S(2)}) copy-start(bf16[512,16,128]{2,1,0:T(8,128)(2,1)} %q_ref.1) | copy-start | bytes 6291460

commit v4 on v3

--- a/solution.py
+++ b/solution.py
@@ -65,6 +65,7 @@
 
 
 SLOTS = 4
+VMEM_BYTES = 62 * 1024 * 1024
 MESH = pl.DeviceIdType.MESH
 
 
@@ -104,6 +105,8 @@
     win_send,
     win_recv,
     load_sem,
+    near_buf,
+    near_sem,
 ):
     count = lax.axis_size("ctx")
     head_count = lax.axis_size("head")
@@ -264,14 +267,24 @@
                 rows_n = kv_ref[base + rows + n * block : base + rows + (n + 1) * block, :]
                 packed = jnp.where(places[n] == s, rows_n.astype(F32), packed)
             stage[target, s * block : (s + 1) * block, :] = packed.astype(BF16)
-        data_copy(me, target).start()
         return carry
 
     lax.fori_loop(0, count - 2 - me, pack, 0)
+
+    @pl.when(me > 0)
+    def _():
+        window_copy(me).wait_recv()
 
     @pl.when(me < count - 1)
     def _():
         list_copy(me + 1, me).wait_recv()
+        window_copy(me + 1).wait_send()
+
+    def send(step, carry):
+        data_copy(me, count - 1 - step).start()
+        return carry
+
+    lax.fori_loop(0, count - 2 - me, send, 0)
 
     mine = sel_ref[...]
     query = lax.broadcasted_iota(jnp.int32, mine.shape, 0) + me * blocks
@@ -298,16 +311,15 @@
     logit_ref[...] = total.T
 
     each(0, me, lambda j: sums_copy(j, me).wait_recv())
-
-    @pl.when(me > 0)
-    def _():
-        window_copy(me).wait_recv()
-
     sums = sums_ref[...].reshape(ck_ref.shape)
     ck_ref[...] = split(sums[:, :width])
     cv_ref[...] = split(sums[:, width:])
     loads[3].wait()
     tokens = 32
+
+    def near_copy(n):
+        at = pl.ds(pl.multiple_of(n * block, block), block)
+        return pltpu.make_async_copy(near_buf.at[at], near_ref.at[at], near_sem.at[n])
 
     def near(n, carry):
         start = base + rows + n * block - WINDOW_TOKENS
@@ -328,7 +340,8 @@
                 heads,
                 block,
             )
-            near_ref[at] = result.reshape(tokens, heads, width)
+            near_buf[at] = result.reshape(tokens, heads, width)
+        near_copy(n).start()
         return carry
 
     lax.fori_loop(0, blocks, near, 0)
@@ -336,10 +349,7 @@
     each(0, me, lambda j: list_copy(me, j).wait_send())
     each(me + 1, count, lambda j: sums_copy(me, j).wait_send())
     each(me + 2, count, lambda j: data_copy(me, j).wait_send())
-
-    @pl.when(me < count - 1)
-    def _():
-        window_copy(me + 1).wait_send()
+    each(0, blocks, lambda n: near_copy(n).wait())
 
     for off in range(1, head_count):
         part_copy(my_head, lax.rem(my_head + off, head_count)).wait_send()
@@ -364,7 +374,7 @@
             jax.ShapeDtypeStruct(padded, jnp.int32),
         ),
         in_specs=[far, whole, far, far, whole, whole, whole, far],
-        out_specs=(whole,) * 4,
+        out_specs=(whole, far, whole, whole),
         scratch_shapes=[
             pltpu.VMEM(hidden.shape, BF16),
             pltpu.VMEM(queries.shape, BF16),
@@ -389,9 +399,11 @@
             dma,
             dma,
             dma((4,)),
+            pltpu.VMEM(queries.shape, F32),
+            dma((blocks,)),
         ],
         compiler_params=pltpu.CompilerParams(
-            collective_id=0, has_side_effects=True, vmem_limit_bytes=48 * 1024 * 1024
+            collective_id=0, has_side_effects=True, vmem_limit_bytes=VMEM_BYTES
         ),
         cost_estimate=pl.CostEstimate(
             flops=3_000_000_000, bytes_accessed=6_000_000, transcendentals=5_000_000
@@ -410,17 +422,17 @@
     k_sel[0:block, :] = own_rows[:, :width]
     v_sel[0:block, :width] = own_rows[:, width:]
     v_sel[0:block, width:] = jnp.ones((block, width), BF16)
-    own_key = jnp.broadcast_to(own_rows[0:1, :width].astype(F32), (block, width))
+    own_key = jnp.broadcast_to(own_rows[0:1, :width].astype(F32), (block, width)).astype(BF16)
     for k in range(1, picked):
         slot = slot_ref[num, k]
-        keep = jnp.where(slot >= 0, 1.0, 0.0)
-        start = pl.multiple_of(jnp.maximum(slot, 0) * block, block)
-        rows = kv_ref[pl.ds(start, block), :].astype(F32)
+        keep = jnp.full((block, width), jnp.where(slot >= 0, 1.0, 0.0), F32).astype(BF16)
+        start = pl.multiple_of(jnp.where(slot >= 0, slot * block, own_start), block)
+        rows = kv_ref[pl.ds(start, block), :]
         at = slice(k * block, (k + 1) * block)
-        k_sel[at, :] = (jnp.where(keep > 0, rows[:, :width], own_key)).astype(BF16)
-        v_sel[at, :width] = jnp.where(keep > 0, rows[:, width:], 0.0).astype(BF16)
-        v_sel[at, width:] = jnp.full((block, width), keep, F32).astype(BF16)
-    tokens = 64
+        k_sel[at, :] = rows[:, :width] * keep + own_key * (1.0 - keep)
+        v_sel[at, :width] = rows[:, width:] * keep
+        v_sel[at, width:] = keep
+    tokens = 32
     rows_n = tokens * heads
     for c in range(block // tokens):
         at = slice(c * tokens, (c + 1) * tokens)
@@ -460,7 +472,7 @@
             pltpu.VMEM((picked * block, width), BF16),
             pltpu.VMEM((picked * block, 2 * width), BF16),
         ],
-        compiler_params=pltpu.CompilerParams(vmem_limit_bytes=48 * 1024 * 1024),
+        compiler_params=pltpu.CompilerParams(vmem_limit_bytes=VMEM_BYTES),
         cost_estimate=pl.CostEstimate(
             flops=4_500_000_000, bytes_accessed=8_000_000, transcendentals=9_000_000
         ),

time: 67.7 us -> 55.5 us (0.82)
  the two profiles are of different devices: /device:TPU:24 before, /device:TPU:21 now
where the time goes in v4:
time: 55.5 us; the launch traced here: 55.4 us
  Pallas kernels  55.4 us (100%)
    pallas_call x1, Pallas kernels, exchange(): pl.pallas_call(exchange_kernel, out_shape=(jax.ShapeDtypeStruct((count *...  36.4 us
    pallas_call x1, Pallas kernels, selected(): pl.pallas_call(selected_kernel, grid=(blocks_here,), out_shape=jax.ShapeD...  19 us

profile of v4, /device:TPU:21, one launch (start us, length us, event | category | flops | bytes accessed | tf_op | source)
XLA Modules:
  0.0 55.4 jit_solution(7052747436833835200)
XLA Ops:
  0.0 36.4 %shard_map.82 = (bf16[3072,256]{1,0:T(8,128)(2,1)}, f32[512,16,128]{2,1,0:T(8,128)}, f32[512,48]{1,0:T(8,128)}, s32[8,128]{1,0:T(8,128)}) custom-call(bf16[512,1792]{1,0:T(8,128)(2,1)} %hidden_ref.1, bf16[192,1792]{1,0:T(8,128)(2,1)} %bitcast.4, bf16[512,128]{1,0:T(8,128)(2,1)} %bitcast.5, bf16[512,128]{1,0:T(8,128)(2,1)} %bitcast.6, ...), custom_call_target="tpu_custom_call" | custom-call | flops 3000000000 | bytes 6000000 | tf_op jit(solution)/shard_map/pallas_call | solution.py:368
  36.4 19.0 %shard_map.83 = bf16[512,16,128]{2,1,0:T(8,128)(2,1)} custom-call(s32[8,128]{1,0:T(8,128)} %get-tuple-element.9.slot_ref, bf16[512,16,128]{2,1,0:T(8,128)(2,1)} %q_ref.1, bf16[3072,256]{1,0:T(8,128)(2,1)} %get-tuple-element.10.kv_ref, f32[512,16,128]{2,1,0:T(8,128)} %get-tuple-element.11.near_ref, f32[512,48]{1,0:T(8,128)} %get-tuple-element.12.logit_ref), custom_call_target="tpu_custom_call" | custom-call | flops 4499999744 | bytes 8000000 | tf_op jit(solution)/shard_map/pallas_call | solution.py:459

commit v5 on v4

--- a/solution.py
+++ b/solution.py
@@ -242,13 +242,6 @@
 
     each(me + 1, count, lambda j: sums_copy(me, j).start())
 
-    loads[2].wait()
-    logits = dot_t(weight_ref[...], hidden[...])
-    for h in range(head_count):
-        partial[h] = logits[h * columns : (h + 1) * columns, :]
-    for off in range(1, head_count):
-        part_copy(my_head, lax.rem(my_head + off, head_count)).start()
-
     def pack(step, carry):
         target = count - 1 - step
         list_copy(target, me).wait_recv()
@@ -262,18 +255,15 @@
             places.append(jnp.where(need > 0, rank, -1.0))
             rank = rank + need
         for s in range(SLOTS):
-            packed = jnp.zeros((block, 2 * width), F32)
+            packed = jnp.zeros((block, 2 * width), BF16)
             for n in range(blocks):
                 rows_n = kv_ref[base + rows + n * block : base + rows + (n + 1) * block, :]
-                packed = jnp.where(places[n] == s, rows_n.astype(F32), packed)
-            stage[target, s * block : (s + 1) * block, :] = packed.astype(BF16)
+                chosen = jnp.where(places[n] == s, 1.0, 0.0)
+                packed += rows_n * jnp.broadcast_to(chosen, rows_n.shape).astype(BF16)
+            stage[target, s * block : (s + 1) * block, :] = packed
         return carry
 
     lax.fori_loop(0, count - 2 - me, pack, 0)
-
-    @pl.when(me > 0)
-    def _():
-        window_copy(me).wait_recv()
 
     @pl.when(me < count - 1)
     def _():
@@ -285,6 +275,13 @@
         return carry
 
     lax.fori_loop(0, count - 2 - me, send, 0)
+
+    loads[2].wait()
+    logits = dot_t(weight_ref[...], hidden[...])
+    for h in range(head_count):
+        partial[h] = logits[h * columns : (h + 1) * columns, :]
+    for off in range(1, head_count):
+        part_copy(my_head, lax.rem(my_head + off, head_count)).start()
 
     mine = sel_ref[...]
     query = lax.broadcasted_iota(jnp.int32, mine.shape, 0) + me * blocks
@@ -311,6 +308,10 @@
     logit_ref[...] = total.T
 
     each(0, me, lambda j: sums_copy(j, me).wait_recv())
+    @pl.when(me > 0)
+    def _():
+        window_copy(me).wait_recv()
+
     sums = sums_ref[...].reshape(ck_ref.shape)
     ck_ref[...] = split(sums[:, :width])
     cv_ref[...] = split(sums[:, width:])

time: 55.5 us -> 59.2 us (1.067)
  the two profiles are of different devices: /device:TPU:21 before, /device:TPU:24 now
where the time goes in v5:
time: 59.2 us; the launch traced here: 59.1 us
  Pallas kernels  59 us (100%)
    pallas_call x1, Pallas kernels, exchange(): pl.pallas_call(exchange_kernel, out_shape=(jax.ShapeDtypeStruct((count *...  40.1 us
    pallas_call x1, Pallas kernels, selected(): pl.pallas_call(selected_kernel, grid=(blocks_here,), out_shape=jax.ShapeD...  19 us

profile of v5, /device:TPU:24, one launch (start us, length us, event | category | flops | bytes accessed | tf_op | source)
XLA Modules:
  0.0 59.1 jit_solution(4058184449528359848)
XLA Ops:
  0.0 40.1 %shard_map.82 = (bf16[3072,256]{1,0:T(8,128)(2,1)}, f32[512,16,128]{2,1,0:T(8,128)}, f32[512,48]{1,0:T(8,128)}, s32[8,128]{1,0:T(8,128)}) custom-call(bf16[512,1792]{1,0:T(8,128)(2,1)} %hidden_ref.1, bf16[192,1792]{1,0:T(8,128)(2,1)} %bitcast.4, bf16[512,128]{1,0:T(8,128)(2,1)} %bitcast.5, bf16[512,128]{1,0:T(8,128)(2,1)} %bitcast.6, ...), custom_call_target="tpu_custom_call" | custom-call | flops 3000000000 | bytes 6000000 | tf_op jit(solution)/shard_map/pallas_call | solution.py:369
  40.1 19.0 %shard_map.83 = bf16[512,16,128]{2,1,0:T(8,128)(2,1)} custom-call(s32[8,128]{1,0:T(8,128)} %get-tuple-element.9.slot_ref, bf16[512,16,128]{2,1,0:T(8,128)(2,1)} %q_ref.1, bf16[3072,256]{1,0:T(8,128)(2,1)} %get-tuple-element.10.kv_ref, f32[512,16,128]{2,1,0:T(8,128)} %get-tuple-element.11.near_ref, f32[512,48]{1,0:T(8,128)} %get-tuple-element.12.logit_ref), custom_call_target="tpu_custom_call" | custom-call | flops 4499999744 | bytes 8000000 | tf_op jit(solution)/shard_map/pallas_call | solution.py:460

commit v6 on v4

--- a/solution.py
+++ b/solution.py
@@ -262,11 +262,12 @@
             places.append(jnp.where(need > 0, rank, -1.0))
             rank = rank + need
         for s in range(SLOTS):
-            packed = jnp.zeros((block, 2 * width), F32)
+            packed = jnp.zeros((block, 2 * width), BF16)
             for n in range(blocks):
                 rows_n = kv_ref[base + rows + n * block : base + rows + (n + 1) * block, :]
-                packed = jnp.where(places[n] == s, rows_n.astype(F32), packed)
-            stage[target, s * block : (s + 1) * block, :] = packed.astype(BF16)
+                chosen = jnp.where(places[n] == s, 1.0, 0.0)
+                packed += rows_n * jnp.broadcast_to(chosen, rows_n.shape).astype(BF16)
+            stage[target, s * block : (s + 1) * block, :] = packed
         return carry
 
     lax.fori_loop(0, count - 2 - me, pack, 0)

time: 55.5 us -> 55.5 us (level)
  no operation moved by 1% of the time
where the time goes in v6:
time: 55.5 us; the launch traced here: 55.4 us
  Pallas kernels  55.4 us (100%)
    pallas_call x1, Pallas kernels, exchange(): pl.pallas_call(exchange_kernel, out_shape=(jax.ShapeDtypeStruct((count *...  36.4 us
    pallas_call x1, Pallas kernels, selected(): pl.pallas_call(selected_kernel, grid=(blocks_here,), out_shape=jax.ShapeD...  19 us

profile of v6, /device:TPU:21, one launch (start us, length us, event | category | flops | bytes accessed | tf_op | source)
XLA Modules:
  0.0 55.4 jit_solution(10856249623757418102)
XLA Ops:
  0.0 36.4 %shard_map.82 = (bf16[3072,256]{1,0:T(8,128)(2,1)}, f32[512,16,128]{2,1,0:T(8,128)}, f32[512,48]{1,0:T(8,128)}, s32[8,128]{1,0:T(8,128)}) custom-call(bf16[512,1792]{1,0:T(8,128)(2,1)} %hidden_ref.1, bf16[192,1792]{1,0:T(8,128)(2,1)} %bitcast.4, bf16[512,128]{1,0:T(8,128)(2,1)} %bitcast.5, bf16[512,128]{1,0:T(8,128)(2,1)} %bitcast.6, ...), custom_call_target="tpu_custom_call" | custom-call | flops 3000000000 | bytes 6000000 | tf_op jit(solution)/shard_map/pallas_call | solution.py:369
  36.4 19.0 %shard_map.83 = bf16[512,16,128]{2,1,0:T(8,128)(2,1)} custom-call(s32[8,128]{1,0:T(8,128)} %get-tuple-element.9.slot_ref, bf16[512,16,128]{2,1,0:T(8,128)(2,1)} %q_ref.1, bf16[3072,256]{1,0:T(8,128)(2,1)} %get-tuple-element.10.kv_ref, f32[512,16,128]{2,1,0:T(8,128)} %get-tuple-element.11.near_ref, f32[512,48]{1,0:T(8,128)} %get-tuple-element.12.logit_ref), custom_call_target="tpu_custom_call" | custom-call | flops 4499999744 | bytes 8000000 | tf_op jit(solution)/shard_map/pallas_call | solution.py:460
